TPU v7x, 256 devices: a whole 4x4x8 slice. The times are simulated.
256 devices in a mesh: row: 16 (over y_lo, x, core), col: 16 (over y_hi, z).
Axes of the slice: x: 4, y: 4 (y_hi: 2, y_lo: 2; y = y_hi * 2 + y_lo), z: 8, core: 2. Of those that a mesh axis runs over, the one named last changes fastest.
Arguments:
- start_modes: float32 [32, 131072], P(None, ('row', 'col')), may hold values from -6 to 6
- energies: float32 [131072], P(('row', 'col')), may hold values from -0.5 to 0.5
- coupling: float32 [2048, 80, 4096], P('row', 'col'), may hold values from -0.0390625 to 0.0390625
- pattern: int32 [2048, 80], P('row', 'col'), may hold values from 0 to 2047, as said below
Outputs:
- filtered: float32 [32, 131072], P(None, ('row', 'col'))
- previous: float32 [32, 131072], P(None, ('row', 'col'))
Inputs may be any that keep to these rules, and one draw needn't show every extreme that they name: In block row i, the 5 entries pattern[i, c * 5] to pattern[i, c * 5 + 4] are distinct block columns j with (j // 8) % 16 == c.
All inputs are finite; a program needn't handle non-finite values.
Results may differ from a plain program's by a relative error of at most 0.0001.
Values sent between devices are 32-bit elements; how exact they have to be, the bound alone decides.
No kernel may reach another device: no remote copies, remote signals or barrier semaphores. Data moves between devices by JAX's collectives and lax.ppermute only.
A program may use at most 128 MiB of HBM per device.

v0:
```python
import jax
import jax.numpy as jnp
from jax import lax
from jax.sharding import PartitionSpec as P

BLOCK = 64
DEGREE = 3


def shards(start_modes, energies, coupling, pattern):
    col_count = lax.axis_size("col")
    mode_count, piece_len = start_modes.shape
    per_piece = piece_len // BLOCK
    rows_here, slot_count = pattern.shape
    piece_ids = pattern // per_piece
    places = piece_ids // col_count * per_piece + pattern % per_piece
    block_mats = coupling.reshape(rows_here, slot_count, BLOCK, BLOCK)

    def coupled(gathered, row_count):
        blocks = gathered.reshape(mode_count, -1, BLOCK)
        sub_mats = block_mats
        picked = jnp.take(blocks, places.reshape(-1), axis=1).reshape(
            mode_count, row_count, per_piece, slot_count, BLOCK
        )
        sub_mats = sub_mats.reshape(row_count, per_piece, slot_count, BLOCK, BLOCK)
        result = jnp.einsum("mqksb,qksab->qmka", picked, sub_mats, precision=lax.Precision.HIGHEST)
        return result.reshape(row_count, mode_count, per_piece * BLOCK)

    def operate(vector):
        gathered = lax.all_gather(vector, "row", axis=1, tiled=True)
        shares_row = lax.psum_scatter(
            coupled(gathered, col_count), "col", scatter_dimension=0, tiled=True
        )[0]
        return energies[None, :] * vector + shares_row

    previous = start_modes
    current = operate(start_modes)
    for degree in range(DEGREE - 1):
        upcoming = 2.0 * operate(current) - previous
        previous = current
        current = upcoming
    return (current, previous)


def solution(mesh):
    in_specs = (P(None, ("row", "col")), P(("row", "col")), P("row", "col", None), P("row", "col"))
    out_specs = (P(None, ("row", "col")), P(None, ("row", "col")))
    return jax.shard_map(shards, mesh=mesh, in_specs=in_specs, out_specs=out_specs, check_vma=False)
```

profile of v0, /device:TPU:2, one launch (start us, length us, event | category | flops | bytes accessed | tf_op | source)
XLA Modules:
  0.0 871.0 jit_solution(7163049960349968008)
XLA Ops:
  7.9 0.7 fusion.21
  9.0 17.4 %reshape_reshape.2 = f32[16,8,5,64,64]{4,3,1,0,2:T(8,128)} reshape(f32[128,5,4096]{2,0,1:T(8,128)} %param.8) | data formatting | bytes 20971520 | tf_op jit(solution)/shard_map/reshape;reshape | solution.py:25
  26.4 21.0 %all-gather.4.cloned.1.call-done = f32[32,8192]{1,0:T(8,128)} async-done(((f32[32,512]{1,0:T(8,128)}), f32[32,8192]{1,0:T(8,128)}) %all-gather.4.cloned.1.call-update) | async-done | bytes 1048592 | tf_op jit(solution)/shard_map/all_gather | solution.py:30
  47.4 3.1 reshape.42
  50.5 2.8 copy.13
  53.3 5.1 gather_fusion
  58.5 9.9 %broadcast_select_fusion.2 = f32[640,32,64]{2,1,0:T(8,128)} fusion(f32[640,32,64]{2,1,0:T(8,128)} %gather_fusion, pred[640]{0:T(1024)(128)(4,1)S(1)} %compare_and_fusion), kind=kLoop, calls=%fused_computation.11 | loop fusion | flops 1310720 | bytes 10486400 | tf_op jit(solution)/shard_map/jit(_take)/select_n | solution.py:22
  68.3 24.8 %fusion.6 = f32[16,32,8,64]{3,1,2,0:T(8,128)S(1)} fusion(f32[32,16,8,5,64]{4,0,3,2,1:T(8,128)} %bitcast.50, f32[16,8,5,64,64]{4,3,1,0,2:T(8,128)} %reshape_reshape.2), kind=kOutput, calls=%fused_computation.12 | convolution fusion | flops 1006632960 | bytes 16777216 | tf_op jit(solution)/shard_map/mqksb,qksab->qmka/dot_general | solution.py:26
  93.1 1.6 copy.15
  94.8 1.5 reshape.45
  96.5 199.4 %reduce-scatter.4.cloned.1.call-done = f32[1,32,512]{2,1,0:T(8,128)} async-done(((f32[16,32,512]{2,1,0:T(8,128)}), f32[1,32,512]{2,1,0:T(8,128)}) %reduce-scatter.4.cloned.1.call-update) | async-done | bytes 65552 | tf_op jit(solution)/shard_map/reduce_scatter | solution.py:31
  295.9 1.5 bitcast_add_fusion.2
  297.4 33.5 %all-gather.6.cloned.1.call-done = f32[32,8192]{1,0:T(8,128)} async-done(((f32[32,512]{1,0:T(8,128)}), f32[32,8192]{1,0:T(8,128)}) %all-gather.6.cloned.1.call-update) | async-done | bytes 1048592 | tf_op jit(solution)/shard_map/all_gather | solution.py:30
  330.9 3.1 reshape.46
  334.0 2.8 copy.16
  336.8 5.1 gather_fusion.1
  341.9 9.9 %broadcast_select_fusion.1 = f32[640,32,64]{2,1,0:T(8,128)} fusion(f32[640,32,64]{2,1,0:T(8,128)} %gather_fusion.1, pred[640]{0:T(1024)(128)(4,1)S(1)} %compare_and_fusion), kind=kLoop, calls=%fused_computation.10 | loop fusion | flops 1310720 | bytes 10486400 | tf_op jit(solution)/shard_map/jit(_take)/select_n | solution.py:22
  351.8 24.8 %fusion.9 = f32[16,32,8,64]{3,1,2,0:T(8,128)S(1)} fusion(f32[32,16,8,5,64]{4,0,3,2,1:T(8,128)} %bitcast.51, f32[16,8,5,64,64]{4,3,1,0,2:T(8,128)} %reshape_reshape.2), kind=kOutput, calls=%fused_computation.13 | convolution fusion | flops 1006632960 | bytes 16777216 | tf_op jit(solution)/shard_map/mqksb,qksab->qmka/dot_general | solution.py:26
  376.6 1.6 copy.18
  378.2 1.5 reshape.48
  379.7 199.6 %reduce-scatter.6.cloned.1.call-done = f32[1,32,512]{2,1,0:T(8,128)} async-done(((f32[16,32,512]{2,1,0:T(8,128)}), f32[1,32,512]{2,1,0:T(8,128)}) %reduce-scatter.6.cloned.1.call-update) | async-done | bytes 65552 | tf_op jit(solution)/shard_map/reduce_scatter | solution.py:31
  579.3 1.5 fusion.18
  581.1 33.1 %all-gather.8.cloned.1.call-done = f32[32,8192]{1,0:T(8,128)} async-done(((f32[32,512]{1,0:T(8,128)}), f32[32,8192]{1,0:T(8,128)}) %all-gather.8.cloned.1.call-update) | async-done | bytes 1048592 | tf_op jit(solution)/shard_map/all_gather | solution.py:30
  614.2 3.1 reshape.49
  617.3 2.8 copy.19
  620.1 5.1 gather_fusion.2
  625.2 9.9 %broadcast_select_fusion = f32[640,32,64]{2,1,0:T(8,128)} fusion(f32[640,32,64]{2,1,0:T(8,128)} %gather_fusion.2, pred[640]{0:T(1024)(128)(4,1)S(1)} %compare_and_fusion), kind=kLoop, calls=%fused_computation.9 | loop fusion | flops 1310720 | bytes 10486400 | tf_op jit(solution)/shard_map/jit(_take)/select_n | solution.py:22
  635.1 24.8 %fusion.12 = f32[16,32,8,64]{3,1,2,0:T(8,128)S(1)} fusion(f32[32,16,8,5,64]{4,0,3,2,1:T(8,128)} %bitcast.49, f32[16,8,5,64,64]{4,3,1,0,2:T(8,128)} %reshape_reshape.2), kind=kOutput, calls=%fused_computation.14 | convolution fusion | flops 1006632960 | bytes 16777216 | tf_op jit(solution)/shard_map/mqksb,qksab->qmka/dot_general | solution.py:26
  659.9 1.6 copy.21
  661.5 1.5 reshape.51
  663.0 199.6 %reduce-scatter.8.cloned.1.call-done = f32[1,32,512]{2,1,0:T(8,128)} async-done(((f32[16,32,512]{2,1,0:T(8,128)}), f32[1,32,512]{2,1,0:T(8,128)}) %reduce-scatter.8.cloned.1.call-update) | async-done | bytes 65552 | tf_op jit(solution)/shard_map/reduce_scatter | solution.py:31
  862.6 1.5 fusion.16
  (25 shorter events, 1.8 us)
Async XLA Ops:
  7.2 40.3 %all-gather.4.cloned.1.call-start = ((), (), s32[]{:S(2)}) async-start(), calls=%async_computation.3 | async-start | bytes 1114112 | tf_op jit(solution)/shard_map/all_gather | solution.py:30
  7.9 288.0 %reduce-scatter.4.cloned.1.call-start = ((), (), s32[]{:S(2)}) async-start(), calls=%async_computation.4 | async-start | bytes 1114112 | tf_op jit(solution)/shard_map/reduce_scatter | solution.py:31
  68.3 227.5 %copy-start.1 = (f32[32,512]{1,0:T(8,128)S(1)}, f32[32,512]{1,0:T(8,128)}, u32[]{:S(2)}) copy-start(f32[32,512]{1,0:T(8,128)} %param.6) | copy-start | bytes 196612
  68.3 227.5 %copy-start.3 = (f32[512]{0:T(512)S(1)}, f32[512]{0:T(512)}, u32[]{:S(2)}) copy-start(f32[512]{0:T(512)} %param.7) | copy-start | bytes 6148
  96.2 234.6 %all-gather.6.cloned.1.call-start = ((), (), s32[]{:S(2)}) async-start(), calls=%async_computation.5 | async-start | bytes 1114112 | tf_op jit(solution)/shard_map/all_gather | solution.py:30
  297.4 282.0 %reduce-scatter.6.cloned.1.call-start = ((), (), s32[]{:S(2)}) async-start(), calls=%async_computation.6 | async-start | bytes 1114112 | tf_op jit(solution)/shard_map/reduce_scatter | solution.py:31
  351.8 227.5 %copy-start = (f32[32,512]{1,0:T(8,128)S(1)}, f32[32,512]{1,0:T(8,128)}, u32[]{:S(2)}) copy-start(f32[32,512]{1,0:T(8,128)} %bitcast_add_fusion.2) | copy-start | bytes 196612
  379.7 234.5 %all-gather.8.cloned.1.call-start = ((), (), s32[]{:S(2)}) async-start(), calls=%async_computation.7 | async-start | bytes 1114112 | tf_op jit(solution)/shard_map/all_gather | solution.py:30
  580.8 281.8 %reduce-scatter.8.cloned.1.call-start = ((), (), s32[]{:S(2)}) async-start(), calls=%async_computation.8 | async-start | bytes 1114112 | tf_op jit(solution)/shard_map/reduce_scatter | solution.py:31
  635.1 227.5 %copy-start.2 = (f32[32,512]{1,0:T(8,128)S(1)}, f32[32,512]{1,0:T(8,128)}, u32[]{:S(2)}) copy-start(f32[32,512]{1,0:T(8,128)} %fusion.18) | copy-start | bytes 196612
Sparse Core Ops, SparseCore 0:
  9.8 37.5 all-gather.3
  96.4 199.4 reduce-scatter.3
  298.2 32.5 all-gather.5
  379.8 199.4 reduce-scatter.5
  581.5 32.5 all-gather.7
  663.1 199.4 reduce-scatter.7
where the time goes:
time: 872 us; the launch traced here: 871 us
  waiting for transfers between devices  687 us (79%)
  matrix products  74.3 us (9%)
  local copies, waits for them, and re-layouts  60.1 us (7%)
  other arithmetic  34.8 us (4%)
  between operations  14.2 us (2%)
    reduce_scatter x3, waiting for transfers between devices, operate(): lax.psum_scatter(coupled(gathered, col_count), 'col', scatter_dimension=0...  599 us
    all_gather x3, waiting for transfers between devices, operate(): gathered = lax.all_gather(vector, 'row', axis=1, tiled=True)  87.6 us
    dot_general x3, matrix products, coupled(): jnp.einsum('mqksb,qksab->qmka', picked, sub_mats, precision=lax.Precision...  74.3 us
    select_n x4, other arithmetic, coupled(): jnp.take(blocks, places.reshape(-1), axis=1)  29.6 us
    reshape x6, local copies, waits for them, and re-layouts, coupled(): blocks = gathered.reshape(mode_count, -1, BLOCK)  17.7 us
  transfers between devices with their start and end apart: 6, of which 6 were waited for; matrix products, arithmetic and copies ran while one was open for 2% of the time, Pallas kernels for 0%

commit v1 on v0

v1 whole, which is shorter than its diff:
```python
import functools

import jax
import jax.numpy as jnp
from jax import lax
from jax.experimental import pallas as pl
from jax.experimental.pallas import tpu as pltpu
from jax.sharding import Mesh
from jax.sharding import PartitionSpec as P

BLOCK = 64
DEGREE = 3
LANES = 128
SUB = 8
SLOTS = 5
PAIRS = (SLOTS + 1) // 2
MODES = 32
PER_PIECE = 8
PIECE = BLOCK * PER_PIECE
TILES = PIECE // LANES
ROWS_HERE = 128
HALF_ROW = BLOCK // 2

Y_LO, X, CORE, Y_HI, Z = 2, 4, 2, 2, 8
ROW_AXES = ("y_lo", "x", "core")
COL_AXES = ("y_hi", "z")
ROW_CHIPS = ("y_lo", "x")


def split(value):
    high = value.astype(jnp.bfloat16)
    low = (value - high.astype(jnp.float32)).astype(jnp.bfloat16)
    return high, low


def left_half(shape):
    return lax.broadcasted_iota(jnp.int32, shape, len(shape) - 1) < BLOCK


def prepare_kernel(raw_ref, out_ref, rows):
    left = left_half((HALF_ROW, LANES))
    zero = jnp.zeros((HALF_ROW, LANES), jnp.float32)
    for row in range(SUB):
        for pair in range(PAIRS):
            first = raw_ref[2 * pair, 0, :, row, :]
            second = raw_ref[2 * pair + 1, 0, :, row, :] if 2 * pair + 1 < SLOTS else None
            if second is None:
                even = jnp.where(left, first, zero)
                odd = jnp.where(left, pltpu.roll(first, BLOCK, 1), zero)
            else:
                even = jnp.where(left, first, pltpu.roll(second, BLOCK, 1))
                odd = jnp.where(left, pltpu.roll(first, BLOCK, 1), second)
            slot = (row * PAIRS + pair) % 2
            rows[slot, pl.ds(0, HALF_ROW, stride=2), :] = even
            rows[slot, pl.ds(1, HALF_ROW, stride=2), :] = odd
            high, low = split(rows[slot])
            lanes = pl.ds(pair * LANES, LANES)
            out_ref[row, 0:BLOCK, lanes] = high
            out_ref[row, BLOCK : 2 * BLOCK, lanes] = low


def prepare(coupling):
    groups = ROWS_HERE // SUB
    raw = coupling.reshape(groups, SUB, SLOTS, HALF_ROW, LANES).transpose(2, 0, 3, 1, 4)
    return pl.pallas_call(
        prepare_kernel,
        grid=(groups,),
        in_specs=[pl.BlockSpec((SLOTS, 1, HALF_ROW, SUB, LANES), lambda g: (0, g, 0, 0, 0))],
        out_specs=pl.BlockSpec((SUB, 2 * BLOCK, PAIRS * LANES), lambda g: (g, 0, 0)),
        out_shape=jax.ShapeDtypeStruct((ROWS_HERE, 2 * BLOCK, PAIRS * LANES), jnp.bfloat16),
        scratch_shapes=[pltpu.VMEM((2, BLOCK, LANES), jnp.float32)],
        name="prepare",
    )(raw)


def apply_kernel(places, mine_ref, other_ref, mats_ref, out_ref, picks):
    group = pl.program_id(0)

    @pl.when(group == 0)
    def _():
        for half, ref in enumerate((mine_ref, other_ref)):
            for chip in range(Y_LO * X):
                for tile in range(TILES):
                    value = ref[chip, :, pl.ds(tile * LANES, LANES)]
                    place = (half * Y_LO * X + chip) * PER_PIECE + 2 * tile
                    for turn, turned in enumerate((value, pltpu.roll(value, BLOCK, 1))):
                        high, low = split(turned)
                        picks[place + turn, 0:MODES, :] = high
                        picks[place + turn, MODES : 2 * MODES, :] = low

    left_picks = left_half((2 * MODES, LANES))
    left_out = left_half((MODES, LANES))
    previous = None
    for row in range(SUB):
        parts = []
        for pair in range(PAIRS):
            first = places[2 * pair, group * SUB + row]
            part = picks[first]
            if 2 * pair + 1 < SLOTS:
                second = places[2 * pair + 1, group * SUB + row]
                part = jnp.where(left_picks, part, picks[second ^ 1])
            parts.append(part)
        product = lax.dot_general(
            jnp.concatenate(parts, axis=1),
            mats_ref[row],
            (((1,), (1,)), ((), ())),
            preferred_element_type=jnp.float32,
        )
        both = product[0:MODES] + product[MODES : 2 * MODES]
        both = both + pltpu.roll(both, BLOCK, 1)
        if row % 2 == 1:
            out_ref[0, :, pl.ds(row // 2 * LANES, LANES)] = jnp.where(left_out, previous, both)
        previous = both


def apply(places, mine, other, mats):
    whole = (Y_LO * X, MODES, PIECE)
    grid_spec = pltpu.PrefetchScalarGridSpec(
        num_scalar_prefetch=1,
        grid=(ROWS_HERE // SUB,),
        in_specs=[
            pl.BlockSpec(whole, lambda g, p: (0, 0, 0)),
            pl.BlockSpec(whole, lambda g, p: (0, 0, 0)),
            pl.BlockSpec((SUB, 2 * BLOCK, PAIRS * LANES), lambda g, p: (g, 0, 0)),
        ],
        out_specs=pl.BlockSpec((1, MODES, PIECE), lambda g, p: (g, 0, 0)),
        scratch_shapes=[pltpu.VMEM((ROWS_HERE, 2 * MODES, LANES), jnp.bfloat16)],
    )
    return pl.pallas_call(
        apply_kernel,
        grid_spec=grid_spec,
        out_shape=jax.ShapeDtypeStruct((Y_HI * Z, MODES, PIECE), jnp.float32),
        name="apply",
    )(places, mine, other, mats)


def swap(value, axis):
    return lax.ppermute(value, axis, [(0, 1), (1, 0)])


def shards(start_modes, energies, coupling, pattern):
    core = lax.axis_index("core")
    y_hi = lax.axis_index("y_hi")
    turned = pattern.T
    piece_row = turned // (PER_PIECE * Y_HI * Z)
    places = (((piece_row % CORE) ^ core) * (Y_LO * X) + piece_row // CORE) * PER_PIECE + turned % PER_PIECE
    mats = prepare(coupling)

    def operate(vector):
        copies = jnp.broadcast_to(vector[None], (Y_LO * X, MODES, PIECE))
        mine = lax.all_to_all(copies, ROW_CHIPS, 0, 0, tiled=False)
        other = swap(mine, "core")
        shares = apply(places, mine, other, mats).reshape(Y_HI, Z, MODES, PIECE)
        away = lax.dynamic_index_in_dim(shares, 1 - y_hi, 0, keepdims=False)
        kept = lax.dynamic_index_in_dim(shares, y_hi, 0, keepdims=False)
        kept = kept + swap(away, "y_hi")
        pieces = lax.all_to_all(kept, "z", 0, 0, tiled=False)
        return energies[None, :] * vector + jnp.sum(pieces, axis=0)

    previous = start_modes
    current = operate(start_modes)
    for degree in range(DEGREE - 1):
        upcoming = 2.0 * operate(current) - previous
        previous = current
        current = upcoming
    return (current, previous)


def solution(mesh):
    fine = Mesh(mesh.devices.reshape(Y_LO, X, CORE, Y_HI, Z), ROW_AXES + COL_AXES)
    both = ROW_AXES + COL_AXES
    in_specs = (P(None, both), P(both), P(ROW_AXES, COL_AXES, None), P(ROW_AXES, COL_AXES))
    out_specs = (P(None, both), P(None, both))
    return jax.shard_map(shards, mesh=fine, in_specs=in_specs, out_specs=out_specs, check_vma=False)
```

time: 872 us -> 234 us (0.27)
  waiting for transfers between devices: 687 us -> 41.7 us
  blocking collectives: 0 us -> 102 us
  matrix products: 74.3 us -> 0 us
  Pallas kernels: 0 us -> 66.9 us
  local copies, waits for them, and re-layouts: 60.1 us -> 6.6 us
  other arithmetic: 34.8 us -> 4.78 us
  between operations: 14.2 us -> 0.76 us
    reduce_scatter x3 -> x0, waiting for transfers between devices: 599 us -> none  [operate(): lax.psum_scatter(coupled(gathered, col_count), 'col', scatter_dimension=0...]
    all_to_all x0 -> x6, blocking collectives: none -> 102 us  [the longest x3 64.7 us: operate(): pieces = lax.all_to_all(kept, 'z', 0, 0, tiled=False)]
    all_gather x3 -> x0, waiting for transfers between devices: 87.6 us -> none  [operate(): gathered = lax.all_gather(vector, 'row', axis=1, tiled=True)]
    dot_general x3 -> x0, matrix products: 74.3 us -> none  [coupled(): jnp.einsum('mqksb,qksab->qmka', picked, sub_mats, precision=lax.Precision...]
    pallas_call x0 -> x4, Pallas kernels: none -> 66.9 us  [the longest x3 49.7 us: apply(): pl.pallas_call(apply_kernel, grid_spec=grid_spec, out_shape=jax.ShapeDtyp...]
    ppermute x0 -> x6, waiting for transfers between devices: none -> 41.7 us  [swap(): return lax.ppermute(value, axis, [(0, 1), (1, 0)])]
    select_n x4 -> x0, other arithmetic: 29.6 us -> none  [coupled(): jnp.take(blocks, places.reshape(-1), axis=1)]
    reshape x10 -> x0, local copies, waits for them, and re-layouts: 22.3 us -> none  [the longest x6 17.7 us: coupled(): blocks = gathered.reshape(mode_count, -1, BLOCK)]
  transfers between devices with their start and end apart: 6 -> 6, of which waited for: 6 -> 5; matrix products, arithmetic and copies ran while one was open for 2% -> 0% of each run, Pallas kernels for 0% -> 7%
where the time goes in v1:
time: 234 us; the launch traced here: 231 us
  blocking collectives  102 us (44%)
  Pallas kernels  66.9 us (29%)
  waiting for transfers between devices  41.7 us (18%)
  starting transfers between devices  8.9 us (4%)
  local copies, waits for them, and re-layouts  6.6 us (3%)
  other arithmetic  4.78 us (2%)
    all_to_all x3, blocking collectives, operate(): pieces = lax.all_to_all(kept, 'z', 0, 0, tiled=False)  64.7 us
    pallas_call x3, Pallas kernels, apply(): pl.pallas_call(apply_kernel, grid_spec=grid_spec, out_shape=jax.ShapeDtyp...  49.7 us
    ppermute x6, waiting for transfers between devices, swap(): return lax.ppermute(value, axis, [(0, 1), (1, 0)])  41.7 us
    all_to_all x3, blocking collectives, operate(): mine = lax.all_to_all(copies, ROW_CHIPS, 0, 0, tiled=False)  37 us
    pallas_call x1, Pallas kernels, prepare(): pl.pallas_call(prepare_kernel, grid=(groups,), in_specs=[pl.BlockSpec((SL...  17.2 us
    ppermute x6, starting transfers between devices, swap(): return lax.ppermute(value, axis, [(0, 1), (1, 0)])  8.9 us
  transfers between devices with their start and end apart: 6, of which 5 were waited for; matrix products, arithmetic and copies ran while one was open for 0% of the time, Pallas kernels for 7%

profile of v1, /device:TPU:2, one launch (start us, length us, event | category | flops | bytes accessed | tf_op | source)
XLA Modules:
  0.0 231.4 jit_solution(12047869836082638013)
XLA Ops:
  0.6 0.9 broadcast_in_dim.6
  1.5 14.6 %all_to_all.30.mine_ref = f32[8,32,512]{2,1,0:T(8,128)S(1)} all-to-all(f32[8,32,512]{2,1,0:T(8,128)S(1)} %broadcast_in_dim.6), channel_id=1, replica_groups=mesh['y_lo'=2,'x'=4,'core'=2,'y_hi'=2,'z'=8] {'y_lo','x'}, dimensions={0} | all-to-all | bytes 1048576 | tf_op jit(solution)/shard_map/all_to_all | solution.py:151
  16.1 17.2 %prepare.1.mats_ref = bf16[128,128,384]{2,1,0:T(8,128)(2,1)} custom-call(f32[5,16,32,8,128]{4,3,2,1,0:T(8,128)} %bitcast.44), custom_call_target="tpu_custom_call" | custom-call | tf_op jit(solution)/shard_map/prepare/pallas_call | solution.py:65
  33.3 0.6 fusion.5.places
  34.0 0.8 copy-done.5
  34.7 16.6 %apply.3 = f32[16,32,512]{2,1,0:T(8,128)} custom-call(s32[5,128]{1,0:T(8,128)} %fusion.5.places, f32[8,32,512]{2,1,0:T(8,128)} %copy-done, f32[8,32,512]{2,1,0:T(8,128)} %copy-done.5, bf16[128,128,384]{2,1,0:T(8,128)(2,1)} %prepare.1.mats_ref), custom_call_target="tpu_custom_call" | custom-call | tf_op jit(solution)/shard_map/apply/pallas_call | solution.py:129
  51.3 1.1 dynamic-slice_bitcast_fusion.2
  52.4 3.0 %collective-permute-start.1 = (f32[8,32,512]{2,1,0:T(8,128)S(1)}, f32[8,32,512]{2,1,0:T(8,128)S(1)}, u32[]{:S(2)}, u32[]{:S(2)}) collective-permute-start(f32[8,32,512]{2,1,0:T(8,128)S(1)} %dynamic-slice_bitcast_fusion.2), channel_id=1, source_target_pairs={{0,8},{8,0},{1,9},{9,1},{2,10},{10,2},{3,11},{11,3},{4,12},{12,4},... | collective-permute-start | bytes 1572872 | tf_op jit(solution)/shard_map/ppermute | solution.py:138
  55.4 12.7 %collective-permute-done.1 = f32[8,32,512]{2,1,0:T(8,128)S(1)} collective-permute-done((f32[8,32,512]{2,1,0:T(8,128)S(1)}, f32[8,32,512]{2,1,0:T(8,128)S(1)}, u32[]{:S(2)}, u32[]{:S(2)}) %collective-permute-start.1) | collective-permute-done | bytes 524320 | tf_op jit(solution)/shard_map/ppermute | solution.py:138
  68.1 1.1 bitcast_add_fusion.2
  69.2 25.4 %all_to_all.31 = f32[8,32,512]{2,1,0:T(8,128)S(1)} all-to-all(f32[8,32,512]{2,1,0:T(8,128)S(1)} %bitcast_add_fusion.2), channel_id=1, replica_groups=mesh['y_lo'=2,'x'=4,'core'=2,'y_hi'=2,'z'=8] {'z'}, dimensions={0} | all-to-all | bytes 1048576 | tf_op jit(solution)/shard_map/all_to_all | solution.py:157
  94.8 0.1 broadcast_in_dim.7
  94.8 11.2 %all_to_all.32.mine_ref = f32[8,32,512]{2,1,0:T(8,128)S(1)} all-to-all(f32[8,32,512]{2,1,0:T(8,128)S(1)} %broadcast_in_dim.7), channel_id=1, replica_groups=mesh['y_lo'=2,'x'=4,'core'=2,'y_hi'=2,'z'=8] {'y_lo','x'}, dimensions={0} | all-to-all | bytes 1048576 | tf_op jit(solution)/shard_map/all_to_all | solution.py:151
  106.0 1.9 collective-permute-done.2.other_ref
  107.9 0.8 copy-done.7
  108.7 16.6 %apply.4 = f32[16,32,512]{2,1,0:T(8,128)} custom-call(s32[5,128]{1,0:T(8,128)} %fusion.5.places, f32[8,32,512]{2,1,0:T(8,128)} %copy-done.2, f32[8,32,512]{2,1,0:T(8,128)} %copy-done.7, bf16[128,128,384]{2,1,0:T(8,128)(2,1)} %prepare.1.mats_ref), custom_call_target="tpu_custom_call" | custom-call | tf_op jit(solution)/shard_map/apply/pallas_call | solution.py:129
  125.3 1.1 dynamic-slice_bitcast_fusion.1
  126.4 3.0 %collective-permute-start.3 = (f32[8,32,512]{2,1,0:T(8,128)S(1)}, f32[8,32,512]{2,1,0:T(8,128)S(1)}, u32[]{:S(2)}, u32[]{:S(2)}) collective-permute-start(f32[8,32,512]{2,1,0:T(8,128)S(1)} %dynamic-slice_bitcast_fusion.1), channel_id=1, source_target_pairs={{0,8},{8,0},{1,9},{9,1},{2,10},{10,2},{3,11},{11,3},{4,12},{12,4},... | collective-permute-start | bytes 1572872 | tf_op jit(solution)/shard_map/ppermute | solution.py:138
  129.3 12.6 %collective-permute-done.3 = f32[8,32,512]{2,1,0:T(8,128)S(1)} collective-permute-done((f32[8,32,512]{2,1,0:T(8,128)S(1)}, f32[8,32,512]{2,1,0:T(8,128)S(1)}, u32[]{:S(2)}, u32[]{:S(2)}) %collective-permute-start.3) | collective-permute-done | bytes 524320 | tf_op jit(solution)/shard_map/ppermute | solution.py:138
  141.9 1.1 bitcast_add_fusion.1
  143.0 19.7 %all_to_all.33 = f32[8,32,512]{2,1,0:T(8,128)S(1)} all-to-all(f32[8,32,512]{2,1,0:T(8,128)S(1)} %bitcast_add_fusion.1), channel_id=1, replica_groups=mesh['y_lo'=2,'x'=4,'core'=2,'y_hi'=2,'z'=8] {'z'}, dimensions={0} | all-to-all | bytes 1048576 | tf_op jit(solution)/shard_map/all_to_all | solution.py:157
  162.8 0.1 broadcast_in_dim.8
  162.8 11.2 %all_to_all.34.mine_ref = f32[8,32,512]{2,1,0:T(8,128)S(1)} all-to-all(f32[8,32,512]{2,1,0:T(8,128)S(1)} %broadcast_in_dim.8), channel_id=1, replica_groups=mesh['y_lo'=2,'x'=4,'core'=2,'y_hi'=2,'z'=8] {'y_lo','x'}, dimensions={0} | all-to-all | bytes 1048576 | tf_op jit(solution)/shard_map/all_to_all | solution.py:151
  174.1 1.9 collective-permute-done.4.other_ref
  176.0 0.8 copy-done.6
  176.8 16.6 %apply.5 = f32[16,32,512]{2,1,0:T(8,128)} custom-call(s32[5,128]{1,0:T(8,128)} %fusion.5.places, f32[8,32,512]{2,1,0:T(8,128)} %copy-done.1, f32[8,32,512]{2,1,0:T(8,128)} %copy-done.6, bf16[128,128,384]{2,1,0:T(8,128)(2,1)} %prepare.1.mats_ref), custom_call_target="tpu_custom_call" | custom-call | tf_op jit(solution)/shard_map/apply/pallas_call | solution.py:129
  193.3 1.1 dynamic-slice_bitcast_fusion
  194.4 2.9 %collective-permute-start.5 = (f32[8,32,512]{2,1,0:T(8,128)S(1)}, f32[8,32,512]{2,1,0:T(8,128)S(1)}, u32[]{:S(2)}, u32[]{:S(2)}) collective-permute-start(f32[8,32,512]{2,1,0:T(8,128)S(1)} %dynamic-slice_bitcast_fusion), channel_id=1, source_target_pairs={{0,8},{8,0},{1,9},{9,1},{2,10},{10,2},{3,11},{11,3},{4,12},{12,4},... | collective-permute-start | bytes 1572872 | tf_op jit(solution)/shard_map/ppermute | solution.py:138
  197.4 12.6 %collective-permute-done.5 = f32[8,32,512]{2,1,0:T(8,128)S(1)} collective-permute-done((f32[8,32,512]{2,1,0:T(8,128)S(1)}, f32[8,32,512]{2,1,0:T(8,128)S(1)}, u32[]{:S(2)}, u32[]{:S(2)}) %collective-permute-start.5) | collective-permute-done | bytes 524320 | tf_op jit(solution)/shard_map/ppermute | solution.py:138
  210.0 1.1 bitcast_add_fusion
  211.1 19.6 %all_to_all.35 = f32[8,32,512]{2,1,0:T(8,128)S(1)} all-to-all(f32[8,32,512]{2,1,0:T(8,128)S(1)} %bitcast_add_fusion), channel_id=1, replica_groups=mesh['y_lo'=2,'x'=4,'core'=2,'y_hi'=2,'z'=8] {'z'}, dimensions={0} | all-to-all | bytes 1048576 | tf_op jit(solution)/shard_map/all_to_all | solution.py:157
  230.8 0.6 multiply_subtract_fusion
  (26 shorter events, 0.2 us)
Async XLA Ops:
  0.6 32.7 %copy-start.9 = (s32[128,5]{0,1:T(8,128)S(1)}, s32[128,5]{0,1:T(8,128)}, u32[]{:S(2)}) copy-start(s32[128,5]{0,1:T(8,128)} %param.7) | copy-start | bytes 7684
  16.1 17.8 %copy-start = (f32[8,32,512]{2,1,0:T(8,128)}, f32[8,32,512]{2,1,0:T(8,128)S(1)}, u32[]{:S(2)}) copy-start(f32[8,32,512]{2,1,0:T(8,128)S(1)} %all_to_all.30.mine_ref) | copy-start | bytes 1572868
  16.1 17.8 %collective-permute-start = (f32[8,32,512]{2,1,0:T(8,128)S(1)}, f32[8,32,512]{2,1,0:T(8,128)S(1)}, u32[]{:S(2)}, u32[]{:S(2)}) collective-permute-start(f32[8,32,512]{2,1,0:T(8,128)S(1)} %all_to_all.30.mine_ref), channel_id=1, source_target_pairs={{0,16},{16,0},{1,17},{17,1},{2,18},{18,2},{3,19},{19,3},{4,20},{20... | collective-permute-start | bytes 1572872 | tf_op jit(solution)/shard_map/ppermute | solution.py:138
  33.3 61.4 %copy-start.3 = (f32[32,512]{1,0:T(8,128)S(1)}, f32[32,512]{1,0:T(8,128)}, u32[]{:S(2)}) copy-start(f32[32,512]{1,0:T(8,128)} %param.4) | copy-start | bytes 196612
  33.3 61.4 %copy-start.8 = (f32[512]{0:T(512)S(1)}, f32[512]{0:T(512)}, u32[]{:S(2)}) copy-start(f32[512]{0:T(512)} %param.5) | copy-start | bytes 6148
  34.0 0.8 copy-start.5
  52.4 15.7 %collective-permute-start.1 = (f32[8,32,512]{2,1,0:T(8,128)S(1)}, f32[8,32,512]{2,1,0:T(8,128)S(1)}, u32[]{:S(2)}, u32[]{:S(2)}) collective-permute-start(f32[8,32,512]{2,1,0:T(8,128)S(1)} %dynamic-slice_bitcast_fusion.2), channel_id=1, source_target_pairs={{0,8},{8,0},{1,9},{9,1},{2,10},{10,2},{3,11},{11,3},{4,12},{12,4},... | collective-permute-start | bytes 1572872 | tf_op jit(solution)/shard_map/ppermute | solution.py:138
  106.0 1.9 copy-start.2
  106.0 1.9 collective-permute-start.2
  107.9 0.8 copy-start.7
  126.4 15.6 %collective-permute-start.3 = (f32[8,32,512]{2,1,0:T(8,128)S(1)}, f32[8,32,512]{2,1,0:T(8,128)S(1)}, u32[]{:S(2)}, u32[]{:S(2)}) collective-permute-start(f32[8,32,512]{2,1,0:T(8,128)S(1)} %dynamic-slice_bitcast_fusion.1), channel_id=1, source_target_pairs={{0,8},{8,0},{1,9},{9,1},{2,10},{10,2},{3,11},{11,3},{4,12},{12,4},... | collective-permute-start | bytes 1572872 | tf_op jit(solution)/shard_map/ppermute | solution.py:138
  162.8 68.6 %copy-start.4 = (f32[32,512]{1,0:T(8,128)}, f32[32,512]{1,0:T(8,128)S(1)}, u32[]{:S(2)}) copy-start(f32[32,512]{1,0:T(8,128)S(1)} %multiply_subtract_fusion.1) | copy-start | bytes 196612
  174.1 1.9 copy-start.1
  174.1 1.9 collective-permute-start.4
  176.0 0.8 copy-start.6
  194.4 15.5 %collective-permute-start.5 = (f32[8,32,512]{2,1,0:T(8,128)S(1)}, f32[8,32,512]{2,1,0:T(8,128)S(1)}, u32[]{:S(2)}, u32[]{:S(2)}) collective-permute-start(f32[8,32,512]{2,1,0:T(8,128)S(1)} %dynamic-slice_bitcast_fusion), channel_id=1, source_target_pairs={{0,8},{8,0},{1,9},{9,1},{2,10},{10,2},{3,11},{11,3},{4,12},{12,4},... | collective-permute-start | bytes 1572872 | tf_op jit(solution)/shard_map/ppermute | solution.py:138

commit v2 on v0

v2 whole, which is shorter than its diff:
```python
import functools

import jax
import jax.numpy as jnp
from jax import lax
from jax.experimental import pallas as pl
from jax.experimental.pallas import tpu as pltpu
from jax.sharding import Mesh
from jax.sharding import PartitionSpec as P

BLOCK = 64
DEGREE = 3
LANES = 128
SUB = 8
SLOTS = 5
PAIRS = (SLOTS + 1) // 2
DEPTH = SLOTS * BLOCK
MODES = 32
PER_PIECE = 8
PIECE = BLOCK * PER_PIECE
TILES = PIECE // LANES
ROWS_HERE = 128
HALF_ROW = BLOCK // 2
AT_ONCE = 2

Y_LO, X, CORE, Y_HI, Z_HI, Z_LO = 2, 4, 2, 2, 4, 2
CHIPS = Y_LO * X
Z = Z_HI * Z_LO
CHUNKS = Y_HI * Z
EARLY = Z_HI // 2
ROW_AXES = ("y_lo", "x", "core")
COL_AXES = ("y_hi", "z_hi", "z_lo")
IN_VMEM = pl.BlockSpec(memory_space=pltpu.VMEM)
IN_SMEM = pl.BlockSpec(memory_space=pltpu.SMEM)


def kept_in_vmem(*shape, dtype=jnp.float32):
    return pltpu.VMEM(shape, dtype)


def call(kernel, name, in_specs, outs, scratch=(), flops=1_000_000, mebibytes=8, **more):
    return pl.pallas_call(
        kernel,
        in_specs=in_specs,
        out_specs=[IN_VMEM] * len(outs),
        out_shape=list(outs),
        scratch_shapes=list(scratch),
        compiler_params=pltpu.CompilerParams(vmem_limit_bytes=mebibytes << 20),
        cost_estimate=pl.CostEstimate(flops=flops, bytes_accessed=1 << 20, transcendentals=0),
        name=name,
        **more,
    )


def split(value):
    high = value.astype(jnp.bfloat16)
    low = (value - high.astype(jnp.float32)).astype(jnp.bfloat16)
    return high, low


def left_half(shape):
    return lax.broadcasted_iota(jnp.int32, shape, len(shape) - 1) < BLOCK


def prepare_kernel(where, places, raw_ref, out_ref, rows):
    left = left_half((HALF_ROW, LANES))
    down, across = (lax.broadcasted_iota(jnp.int32, (LANES, LANES), dim) for dim in range(2))
    unit = jnp.where(down == across, 1.0, 0.0).astype(jnp.bfloat16)
    for chunk in range(AT_ONCE):
        for row in range(SUB):
            for pair in range(PAIRS):
                first = raw_ref[2 * pair, chunk, :, row, :]
                last = 2 * pair + 1 == SLOTS
                second = first if last else raw_ref[2 * pair + 1, chunk, :, row, :]
                even = jnp.where(left, first, pltpu.roll(second, BLOCK, 1))
                odd = jnp.where(left, pltpu.roll(first, BLOCK, 1), second)
                slot = (chunk * SUB + row) * PAIRS + pair
                rows[slot, pl.ds(0, HALF_ROW, stride=2), :] = even
                rows[slot, pl.ds(1, HALF_ROW, stride=2), :] = odd
                depth = BLOCK if last else LANES
                turned = lax.dot_general(
                    unit[0:depth],
                    jnp.concatenate(split(rows[slot]), axis=0),
                    (((1,), (1,)), ((), ())),
                    preferred_element_type=jnp.float32,
                )
                out_ref[chunk, row, pl.ds(pair * LANES, depth), :] = turned.astype(jnp.bfloat16)


def prepare(where, places, coupling):
    raw = coupling.reshape(CHUNKS, SUB, SLOTS, HALF_ROW, LANES).transpose(2, 0, 3, 1, 4)
    raw = pltpu.with_memory_space_constraint(raw, pltpu.HBM)
    return pl.pallas_call(
        prepare_kernel,
        grid=(CHUNKS // AT_ONCE,),
        in_specs=[IN_SMEM, IN_SMEM, pl.BlockSpec((SLOTS, AT_ONCE, HALF_ROW, SUB, LANES), lambda g: (0, g, 0, 0, 0))],
        out_specs=pl.BlockSpec((AT_ONCE, SUB, DEPTH, LANES), lambda g: (g, 0, 0, 0)),
        out_shape=pltpu.HBM((CHUNKS, SUB, DEPTH, LANES), jnp.bfloat16),
        scratch_shapes=[pltpu.VMEM((AT_ONCE * SUB * PAIRS, BLOCK, LANES), jnp.float32)],
        compiler_params=pltpu.CompilerParams(vmem_limit_bytes=16 << 20),
        cost_estimate=pl.CostEstimate(flops=20_000_000_000, bytes_accessed=21 << 20, transcendentals=0),
        name="prepare",
    )(where, places, raw)


def fill_picks(refs, picks):
    for half, ref in enumerate(refs):
        for chip in range(CHIPS):
            for tile in range(TILES):
                value = ref[chip, :, pl.ds(tile * LANES, LANES)]
                place = (half * CHIPS + chip) * PER_PIECE + 2 * tile
                for turn, turned in enumerate((value, pltpu.roll(value, BLOCK, 1))):
                    high, low = split(turned)
                    picks[place + turn, 0:MODES, :] = high
                    picks[place + turn, MODES : 2 * MODES, :] = low


def multiply(chunks, stores, places, picks, mats):
    left_picks = left_half((2 * MODES, LANES))
    left_out = left_half((MODES, LANES))
    for chunk, store in zip(chunks, stores):
        previous = None
        for offset in range(SUB):
            row = chunk * SUB + offset
            parts = []
            for pair in range(PAIRS):
                part = picks[places[2 * pair, row]]
                if 2 * pair + 1 < SLOTS:
                    parts.append(jnp.where(left_picks, part, picks[places[2 * pair + 1, row] ^ 1]))
                else:
                    parts.append(part[:, 0:BLOCK])
            product = jnp.dot(jnp.concatenate(parts, axis=1), mats[chunk, offset], preferred_element_type=jnp.float32)
            both = product[0:MODES] + product[MODES : 2 * MODES]
            both = both + pltpu.roll(both, BLOCK, 1)
            if offset % 2 == 1:
                store(pl.ds(offset // 2 * LANES, LANES), jnp.where(left_out, previous, both))
            previous = both


def into(ref, *index):
    def store(lanes, value):
        ref[(*index, slice(None), lanes)] = value

    return store


def late_chunks(parity):
    return [(y, a, y * Z + (EARLY + a) * Z_LO + parity) for y in range(Y_HI) for a in range(Z_HI - EARLY)]


def first_kernel(where, places, mine, other, mats, out, picks):
    chunks = [(1 - where[0]) * Z + k for k in range(EARLY * Z_LO)]
    fill_picks((mine, other), picks)
    multiply(chunks, [into(out, k) for k in range(len(chunks))], places, picks, mats)


def second_kernel(where, places, picks, mats, out):
    late = late_chunks(1 - where[1])
    chunks = [chunk for _, _, chunk in late]
    multiply(chunks, [into(out, y, a) for y, a, _ in late], places, picks, mats)


def third_kernel(where, places, picks, mats, early_out, late_out):
    late = late_chunks(where[1])
    chunks = [where[0] * Z + k for k in range(EARLY * Z_LO)]
    stores = [into(early_out, k) for k in range(len(chunks))]
    chunks += [chunk for _, _, chunk in late]
    stores += [into(late_out, y, a) for y, a, _ in late]
    multiply(chunks, stores, places, picks, mats)


def multiplier(kernel, name, inputs, outs, count):
    return call(
        kernel,
        name,
        [IN_SMEM, IN_SMEM] + [IN_VMEM] * (inputs + 1),
        outs,
        flops=count * 400_000_000,
    )


def middle_kernel(where, early_kept, early_got, late_kept, late_got, beside, across, early, late):
    y, parity = where[0], where[1]
    for a in range(EARLY):
        for target, half in ((early, parity), (beside, 1 - parity)):
            target[a] = early_kept[Z_LO * a + half] + early_got[Z_LO * a + half]
    for a in range(Z_HI - EARLY):
        for target, half in ((late, y), (across, 1 - y)):
            target[a] = late_kept[half, a] + late_got[half, a]


def last_kernel(early, beside_got, late, across_got, sums):
    for a in range(EARLY):
        sums[a] = early[a] + beside_got[a]
    for a in range(Z_HI - EARLY):
        sums[EARLY + a] = late[a] + across_got[a]


def finish_kernel(scale, energies, vector, before, pieces, out, copies):
    total = energies[...] * vector[...]
    for chip in range(Z_HI):
        total = total + pieces[chip]
    if scale != 1.0:
        total = scale * total - before[...]
    out[...] = total
    for chip in range(CHIPS):
        copies[chip] = total


def tie_kernel(mine, mats, out):
    pass


def swap(value, axis):
    return lax.ppermute(value, axis, [(0, 1), (1, 0)])


def reduce(where, away, beside, early_kept, late_kept):
    away_got, beside_got = swap(away, "y_hi"), swap(beside, "z_lo")
    piece = kept_in_vmem(EARLY, MODES, PIECE)
    beside, across, early, late = call(middle_kernel, "middle", [IN_SMEM] + [IN_VMEM] * 4, [piece] * 4)(
        where, early_kept, away_got, late_kept, beside_got
    )
    beside_got, across_got = swap(beside, "z_lo"), swap(across, "y_hi")
    [sums] = call(last_kernel, "last", [IN_VMEM] * 4, [kept_in_vmem(Z_HI, MODES, PIECE)])(
        early, beside_got, late, across_got
    )
    return lax.all_to_all(sums, "z_hi", 0, 0, tiled=False)


def shards(start_modes, energies, coupling, pattern):
    core, y_hi, z_lo = (lax.axis_index(name) for name in ("core", "y_hi", "z_lo"))
    turned = pattern.T
    piece_row = turned // (PER_PIECE * CHUNKS)
    places = (((piece_row % CORE) ^ core) * CHIPS + piece_row // CORE) * PER_PIECE + turned % PER_PIECE
    where = jnp.stack([y_hi, z_lo]).astype(jnp.int32)
    mats = prepare(where, places, coupling)
    level = energies[None, :]
    picks_shape = kept_in_vmem(ROWS_HERE, 2 * MODES, LANES, dtype=jnp.bfloat16)
    early_shape = kept_in_vmem(EARLY * Z_LO, MODES, PIECE)
    late_shape = kept_in_vmem(Y_HI, Z_HI - EARLY, MODES, PIECE)

    def operate(copies, tied):
        mine = lax.all_to_all(copies, ("y_lo", "x"), 0, 0, tiled=False)
        if tied:
            [mine] = call(
                tie_kernel, "tie", [IN_VMEM, pl.BlockSpec(memory_space=pl.ANY)], [kept_in_vmem(*mine.shape)], input_output_aliases={0: 0}
            )(mine, pltpu.with_memory_space_constraint(mats, pltpu.HBM))
        other = swap(mine, "core")
        away, picks = multiplier(first_kernel, "first", 2, [early_shape, picks_shape], 4)(where, places, mine, other, mats)
        [beside] = multiplier(second_kernel, "second", 1, [late_shape], 4)(where, places, picks, mats)
        early, late = multiplier(third_kernel, "third", 1, [early_shape, late_shape], 8)(where, places, picks, mats)
        return reduce(where, away, beside, early, late)

    vector_shape = kept_in_vmem(MODES, PIECE)
    previous = before = start_modes
    current = start_modes
    copies = jnp.broadcast_to(start_modes[None], (CHIPS, MODES, PIECE))
    for degree in range(DEGREE):
        pieces = operate(copies, degree == 0)
        finish = functools.partial(finish_kernel, 1.0 if degree == 0 else 2.0)
        upcoming, copies = call(
            finish, "finish", [IN_VMEM] * 4, [vector_shape, kept_in_vmem(CHIPS, MODES, PIECE)]
        )(level, current, before, pieces)
        before = current
        current = upcoming
    return (current, before)


def solution(mesh):
    fine = Mesh(mesh.devices.reshape(Y_LO, X, CORE, Y_HI, Z_HI, Z_LO), ROW_AXES + COL_AXES)
    both = ROW_AXES + COL_AXES
    in_specs = (P(None, both), P(both), P(ROW_AXES, COL_AXES, None), P(ROW_AXES, COL_AXES))
    out_specs = (P(None, both), P(None, both))
    return jax.shard_map(shards, mesh=fine, in_specs=in_specs, out_specs=out_specs, check_vma=False)
```

time: 872 us -> 167 us (0.19)
  waiting for transfers between devices: 687 us -> 44.2 us
  matrix products: 74.3 us -> 0 us
  local copies, waits for them, and re-layouts: 60.1 us -> 4.95 us
  blocking collectives: 0 us -> 52.8 us
  other arithmetic: 34.8 us -> 0.78 us
  Pallas kernels: 0 us -> 33.5 us
  starting transfers between devices: 0.64 us -> 29.3 us
  between operations: 14.2 us -> 0.74 us
    reduce_scatter x3 -> x0, waiting for transfers between devices: 599 us -> none  [operate(): lax.psum_scatter(coupled(gathered, col_count), 'col', scatter_dimension=0...]
    all_gather x3 -> x0, waiting for transfers between devices: 87.6 us -> none  [operate(): gathered = lax.all_gather(vector, 'row', axis=1, tiled=True)]
    dot_general x3 -> x0, matrix products: 74.3 us -> none  [coupled(): jnp.einsum('mqksb,qksab->qmka', picked, sub_mats, precision=lax.Precision...]
    all_to_all x0 -> x4, blocking collectives: none -> 52.8 us  [the longest x2 29.2 us: reduce(): return lax.all_to_all(sums, 'z_hi', 0, 0, tiled=False)]
    ppermute x0 -> x15, waiting for transfers between devices: none -> 35 us  [swap(): return lax.ppermute(value, axis, [(0, 1), (1, 0)])]
    pallas_call x0 -> x20, Pallas kernels: none -> 33.5 us  [the longest x1 14.9 us: prepare(): pl.pallas_call(prepare_kernel, grid=(CHUNKS // AT_ONCE,), in_specs=[IN_SM...]
    select_n x4 -> x0, other arithmetic: 29.6 us -> none  [coupled(): jnp.take(blocks, places.reshape(-1), axis=1)]
    reshape x10 -> x0, local copies, waits for them, and re-layouts: 22.3 us -> none  [the longest x6 17.7 us: coupled(): blocks = gathered.reshape(mode_count, -1, BLOCK)]
  transfers between devices with their start and end apart: 6 -> 17, of which waited for: 6 -> 16; matrix products, arithmetic and copies ran while one was open for 2% -> 1% of each run, Pallas kernels for 0% -> 15%
where the time goes in v2:
time: 167 us; the launch traced here: 166 us
  blocking collectives  52.8 us (32%)
  waiting for transfers between devices  44.2 us (26%)
  Pallas kernels  33.5 us (20%)
  starting transfers between devices  29.3 us (18%)
  local copies, waits for them, and re-layouts  4.95 us (3%)
    ppermute x15, waiting for transfers between devices, swap(): return lax.ppermute(value, axis, [(0, 1), (1, 0)])  35 us
    all_to_all x2, blocking collectives, reduce(): return lax.all_to_all(sums, 'z_hi', 0, 0, tiled=False)  29.2 us
    all_to_all x2, blocking collectives, operate(): mine = lax.all_to_all(copies, ('y_lo', 'x'), 0, 0, tiled=False)  23.5 us
    ppermute x15, starting transfers between devices, swap(): return lax.ppermute(value, axis, [(0, 1), (1, 0)])  20.1 us
    pallas_call x1, Pallas kernels, prepare(): pl.pallas_call(prepare_kernel, grid=(CHUNKS // AT_ONCE,), in_specs=[IN_SM...  14.9 us
    all_to_all x1, waiting for transfers between devices, reduce(): return lax.all_to_all(sums, 'z_hi', 0, 0, tiled=False)  9.21 us
    pallas_call x3, Pallas kernels, operate(): multiplier(third_kernel, 'third', 1, [early_shape, late_shape], 8)  5.89 us
    all_to_all x1, starting transfers between devices, operate(): mine = lax.all_to_all(copies, ('y_lo', 'x'), 0, 0, tiled=False)  5.84 us
  transfers between devices with their start and end apart: 17, of which 16 were waited for; matrix products, arithmetic and copies ran while one was open for 1% of the time, Pallas kernels for 15%

profile of v2, /device:TPU:2, one launch (start us, length us, event | category | flops | bytes accessed | tf_op | source)
XLA Modules:
  0.0 166.2 jit_solution(16221135704323366134)
XLA Ops:
  2.3 5.8 %all-to-all-start = ((f32[8,32,512]{2,1,0:T(8,128)}), f32[8,32,512]{2,1,0:T(8,128)S(1)}, u32[]{:S(2)}, u32[]{:S(2)}) async-start(f32[8,32,512]{2,1,0:T(8,128)} %broadcast_in_dim.10), calls=%async_computation | async-start | bytes 1048576 | tf_op jit(solution)/shard_map/all_to_all | solution.py:244
  9.0 14.9 %prepare.1.mats = bf16[16,8,320,128]{3,2,1,0:T(8,128)(2,1)} custom-call(s32[2]{0:T(128)S(1)} %pad_add_fusion.where, s32[5,128]{1,0:T(8,128)S(1)} %fusion.5.places, f32[5,16,32,8,128]{4,3,2,1,0:T(8,128)} %bitcast.35), custom_call_target="tpu_custom_call" | custom-call | flops 20000000000 | bytes 22020096 | tf_op jit(solution)/shard_map/prepare/pallas_call | solution.py:93
  24.0 1.9 %collective-permute-done.other = f32[8,32,512]{2,1,0:T(8,128)S(1)} collective-permute-done((f32[8,32,512]{2,1,0:T(8,128)S(1)}, f32[8,32,512]{2,1,0:T(8,128)S(1)}, u32[]{:S(2)}, u32[]{:S(2)}) %collective-permute-start) | collective-permute-done | bytes 524320 | tf_op jit(solution)/shard_map/ppermute | solution.py:215
  25.9 2.0 %copy-done = bf16[16,8,320,128]{3,2,1,0:T(8,128)(2,1)S(1)} copy-done((bf16[16,8,320,128]{3,2,1,0:T(8,128)(2,1)S(1)}, bf16[16,8,320,128]{3,2,1,0:T(8,128)(2,1)}, u32[]{:S(2)}) %copy-start) | copy-done | bytes 10485784
  29.5 3.0 %collective-permute-start.1 = (f32[4,32,512]{2,1,0:T(8,128)S(1)}, f32[4,32,512]{2,1,0:T(8,128)S(1)}, u32[]{:S(2)}, u32[]{:S(2)}) collective-permute-start(f32[4,32,512]{2,1,0:T(8,128)S(1)} %get-tuple-element.33), channel_id=1, source_target_pairs={{0,8},{8,0},{1,9},{9,1},{2,10},{10,2},{3,11},{11,3},{4,12},{12,4},... | collective-permute-start | bytes 786440 | tf_op jit(solution)/shard_map/ppermute | solution.py:215
  33.9 2.0 %collective-permute-start.2 = (f32[2,2,32,512]{3,2,1,0:T(8,128)S(1)}, f32[2,2,32,512]{3,2,1,0:T(8,128)S(1)}, u32[]{:S(2)}, u32[]{:S(2)}) collective-permute-start(f32[2,2,32,512]{3,2,1,0:T(8,128)S(1)} %second.3), channel_id=1, source_target_pairs={{0,1},{1,0},{2,3},{3,2},{4,5},{5,4},{6,7},{7,6},{8,9},{9,8},{10,11... | collective-permute-start | bytes 786440 | tf_op jit(solution)/shard_map/ppermute | solution.py:215
  35.9 2.0 %third.3 = (f32[4,32,512]{2,1,0:T(8,128)S(1)}, f32[2,2,32,512]{3,2,1,0:T(8,128)S(1)}) custom-call(s32[2]{0:T(128)S(1)} %pad_add_fusion.where, s32[5,128]{1,0:T(8,128)S(1)} %fusion.5.places, bf16[128,64,128]{2,1,0:T(8,128)(2,1)S(1)} %get-tuple-element.31.picks, bf16[16,8,320,128]{3,2,1,0:T(8,128)(2,1)S(1)} %copy-done), custom_call_target="tpu_custom_call" | custom-call | flops 3200000000 | bytes 1048576 | tf_op jit(solution)/shard_map/third/pallas_call | solution.py:252
  38.6 2.8 %collective-permute-done.2.late_got = f32[2,2,32,512]{3,2,1,0:T(8,128)S(1)} collective-permute-done((f32[2,2,32,512]{3,2,1,0:T(8,128)S(1)}, f32[2,2,32,512]{3,2,1,0:T(8,128)S(1)}, u32[]{:S(2)}, u32[]{:S(2)}) %collective-permute-start.2) | collective-permute-done | bytes 262176 | tf_op jit(solution)/shard_map/ppermute | solution.py:215
  42.0 1.8 %collective-permute-start.3 = (f32[2,32,512]{2,1,0:T(8,128)S(1)}, f32[2,32,512]{2,1,0:T(8,128)S(1)}, u32[]{:S(2)}, u32[]{:S(2)}) collective-permute-start(f32[2,32,512]{2,1,0:T(8,128)S(1)} %get-tuple-element.36), channel_id=1, source_target_pairs={{0,1},{1,0},{2,3},{3,2},{4,5},{5,4},{6,7},{7,6},{8,9},{9,8},{10,11... | collective-permute-start | bytes 393224 | tf_op jit(solution)/shard_map/ppermute | solution.py:215
  44.4 2.6 %collective-permute-done.3.beside_got = f32[2,32,512]{2,1,0:T(8,128)S(1)} collective-permute-done((f32[2,32,512]{2,1,0:T(8,128)S(1)}, f32[2,32,512]{2,1,0:T(8,128)S(1)}, u32[]{:S(2)}, u32[]{:S(2)}) %collective-permute-start.3) | collective-permute-done | bytes 131104 | tf_op jit(solution)/shard_map/ppermute | solution.py:215
  47.0 3.2 %collective-permute-done.4.across_got = f32[2,32,512]{2,1,0:T(8,128)S(1)} collective-permute-done((f32[2,32,512]{2,1,0:T(8,128)S(1)}, f32[2,32,512]{2,1,0:T(8,128)S(1)}, u32[]{:S(2)}, u32[]{:S(2)}) %collective-permute-start.4) | collective-permute-done | bytes 131104 | tf_op jit(solution)/shard_map/ppermute | solution.py:215
  50.3 17.0 %all_to_all.30.pieces = f32[4,32,512]{2,1,0:T(8,128)S(1)} all-to-all(f32[4,32,512]{2,1,0:T(8,128)S(1)} %last.3), channel_id=1, replica_groups=mesh['y_lo'=2,'x'=4,'core'=2,'y_hi'=2,'z_hi'=4,'z_lo'=2] {'z_hi'}, dimensions={0} | all-to-all | bytes 524288 | tf_op jit(solution)/shard_map/all_to_all | solution.py:228
  67.4 12.4 %all_to_all.31.mine = f32[8,32,512]{2,1,0:T(8,128)S(1)} all-to-all(f32[8,32,512]{2,1,0:T(8,128)S(1)} %get-tuple-element.40), channel_id=1, replica_groups=mesh['y_lo'=2,'x'=4,'core'=2,'y_hi'=2,'z_hi'=4,'z_lo'=2] {'y_lo','x'}, dimensions={0} | all-to-all | bytes 1048576 | tf_op jit(solution)/shard_map/all_to_all | solution.py:244
  79.8 1.9 %collective-permute-done.5.other = f32[8,32,512]{2,1,0:T(8,128)S(1)} collective-permute-done((f32[8,32,512]{2,1,0:T(8,128)S(1)}, f32[8,32,512]{2,1,0:T(8,128)S(1)}, u32[]{:S(2)}, u32[]{:S(2)}) %collective-permute-start.5) | collective-permute-done | bytes 524320 | tf_op jit(solution)/shard_map/ppermute | solution.py:215
  83.4 1.9 %collective-permute-start.6 = (f32[4,32,512]{2,1,0:T(8,128)S(1)}, f32[4,32,512]{2,1,0:T(8,128)S(1)}, u32[]{:S(2)}, u32[]{:S(2)}) collective-permute-start(f32[4,32,512]{2,1,0:T(8,128)S(1)} %get-tuple-element.43), channel_id=1, source_target_pairs={{0,8},{8,0},{1,9},{9,1},{2,10},{10,2},{3,11},{11,3},{4,12},{12,4},... | collective-permute-start | bytes 786440 | tf_op jit(solution)/shard_map/ppermute | solution.py:215
  86.7 1.7 %collective-permute-start.7 = (f32[2,2,32,512]{3,2,1,0:T(8,128)S(1)}, f32[2,2,32,512]{3,2,1,0:T(8,128)S(1)}, u32[]{:S(2)}, u32[]{:S(2)}) collective-permute-start(f32[2,2,32,512]{3,2,1,0:T(8,128)S(1)} %second.4), channel_id=1, source_target_pairs={{0,1},{1,0},{2,3},{3,2},{4,5},{5,4},{6,7},{7,6},{8,9},{9,8},{10,11... | collective-permute-start | bytes 786440 | tf_op jit(solution)/shard_map/ppermute | solution.py:215
  88.5 2.0 %third.4 = (f32[4,32,512]{2,1,0:T(8,128)S(1)}, f32[2,2,32,512]{3,2,1,0:T(8,128)S(1)}) custom-call(s32[2]{0:T(128)S(1)} %pad_add_fusion.where, s32[5,128]{1,0:T(8,128)S(1)} %fusion.5.places, bf16[128,64,128]{2,1,0:T(8,128)(2,1)S(1)} %get-tuple-element.41.picks, bf16[16,8,320,128]{3,2,1,0:T(8,128)(2,1)S(1)} %copy-done), custom_call_target="tpu_custom_call" | custom-call | flops 3200000000 | bytes 1048576 | tf_op jit(solution)/shard_map/third/pallas_call | solution.py:252
  90.5 2.9 %collective-permute-done.6.early_got = f32[4,32,512]{2,1,0:T(8,128)S(1)} collective-permute-done((f32[4,32,512]{2,1,0:T(8,128)S(1)}, f32[4,32,512]{2,1,0:T(8,128)S(1)}, u32[]{:S(2)}, u32[]{:S(2)}) %collective-permute-start.6) | collective-permute-done | bytes 262176 | tf_op jit(solution)/shard_map/ppermute | solution.py:215
  93.4 1.7 %collective-permute-done.7.late_got = f32[2,2,32,512]{3,2,1,0:T(8,128)S(1)} collective-permute-done((f32[2,2,32,512]{3,2,1,0:T(8,128)S(1)}, f32[2,2,32,512]{3,2,1,0:T(8,128)S(1)}, u32[]{:S(2)}, u32[]{:S(2)}) %collective-permute-start.7) | collective-permute-done | bytes 262176 | tf_op jit(solution)/shard_map/ppermute | solution.py:215
  98.9 1.8 %collective-permute-done.8.beside_got = f32[2,32,512]{2,1,0:T(8,128)S(1)} collective-permute-done((f32[2,32,512]{2,1,0:T(8,128)S(1)}, f32[2,32,512]{2,1,0:T(8,128)S(1)}, u32[]{:S(2)}, u32[]{:S(2)}) %collective-permute-start.8) | collective-permute-done | bytes 131104 | tf_op jit(solution)/shard_map/ppermute | solution.py:215
  100.7 3.0 %collective-permute-done.9.across_got = f32[2,32,512]{2,1,0:T(8,128)S(1)} collective-permute-done((f32[2,32,512]{2,1,0:T(8,128)S(1)}, f32[2,32,512]{2,1,0:T(8,128)S(1)}, u32[]{:S(2)}, u32[]{:S(2)}) %collective-permute-start.9) | collective-permute-done | bytes 131104 | tf_op jit(solution)/shard_map/ppermute | solution.py:215
  103.8 12.2 %all_to_all.32.pieces = f32[4,32,512]{2,1,0:T(8,128)S(1)} all-to-all(f32[4,32,512]{2,1,0:T(8,128)S(1)} %last.4), channel_id=1, replica_groups=mesh['y_lo'=2,'x'=4,'core'=2,'y_hi'=2,'z_hi'=4,'z_lo'=2] {'z_hi'}, dimensions={0} | all-to-all | bytes 524288 | tf_op jit(solution)/shard_map/all_to_all | solution.py:228
  116.0 11.1 %all_to_all.33.mine = f32[8,32,512]{2,1,0:T(8,128)S(1)} all-to-all(f32[8,32,512]{2,1,0:T(8,128)S(1)} %get-tuple-element.50), channel_id=1, replica_groups=mesh['y_lo'=2,'x'=4,'core'=2,'y_hi'=2,'z_hi'=4,'z_lo'=2] {'y_lo','x'}, dimensions={0} | all-to-all | bytes 1048576 | tf_op jit(solution)/shard_map/all_to_all | solution.py:244
  127.1 1.9 %collective-permute-done.10.other = f32[8,32,512]{2,1,0:T(8,128)S(1)} collective-permute-done((f32[8,32,512]{2,1,0:T(8,128)S(1)}, f32[8,32,512]{2,1,0:T(8,128)S(1)}, u32[]{:S(2)}, u32[]{:S(2)}) %collective-permute-start.10) | collective-permute-done | bytes 524320 | tf_op jit(solution)/shard_map/ppermute | solution.py:215
  130.7 2.5 %collective-permute-start.11 = (f32[4,32,512]{2,1,0:T(8,128)S(1)}, f32[4,32,512]{2,1,0:T(8,128)S(1)}, u32[]{:S(2)}, u32[]{:S(2)}) collective-permute-start(f32[4,32,512]{2,1,0:T(8,128)S(1)} %get-tuple-element.53), channel_id=1, source_target_pairs={{0,8},{8,0},{1,9},{9,1},{2,10},{10,2},{3,11},{11,3},{4,12},{12,4},... | collective-permute-start | bytes 786440 | tf_op jit(solution)/shard_map/ppermute | solution.py:215
  135.6 2.0 %third.5 = (f32[4,32,512]{2,1,0:T(8,128)S(1)}, f32[2,2,32,512]{3,2,1,0:T(8,128)S(1)}) custom-call(s32[2]{0:T(128)S(1)} %pad_add_fusion.where, s32[5,128]{1,0:T(8,128)S(1)} %fusion.5.places, bf16[128,64,128]{2,1,0:T(8,128)(2,1)S(1)} %get-tuple-element.51.picks, bf16[16,8,320,128]{3,2,1,0:T(8,128)(2,1)S(1)} %copy-done), custom_call_target="tpu_custom_call" | custom-call | flops 3200000000 | bytes 1048576 | tf_op jit(solution)/shard_map/third/pallas_call | solution.py:252
  137.5 3.1 %collective-permute-done.11.early_got = f32[4,32,512]{2,1,0:T(8,128)S(1)} collective-permute-done((f32[4,32,512]{2,1,0:T(8,128)S(1)}, f32[4,32,512]{2,1,0:T(8,128)S(1)}, u32[]{:S(2)}, u32[]{:S(2)}) %collective-permute-start.11) | collective-permute-done | bytes 262176 | tf_op jit(solution)/shard_map/ppermute | solution.py:215
  140.7 2.1 %collective-permute-done.12.late_got = f32[2,2,32,512]{3,2,1,0:T(8,128)S(1)} collective-permute-done((f32[2,2,32,512]{3,2,1,0:T(8,128)S(1)}, f32[2,2,32,512]{3,2,1,0:T(8,128)S(1)}, u32[]{:S(2)}, u32[]{:S(2)}) %collective-permute-start.12) | collective-permute-done | bytes 262176 | tf_op jit(solution)/shard_map/ppermute | solution.py:215
  145.5 2.9 %collective-permute-done.13.beside_got = f32[2,32,512]{2,1,0:T(8,128)S(1)} collective-permute-done((f32[2,32,512]{2,1,0:T(8,128)S(1)}, f32[2,32,512]{2,1,0:T(8,128)S(1)}, u32[]{:S(2)}, u32[]{:S(2)}) %collective-permute-start.13) | collective-permute-done | bytes 131104 | tf_op jit(solution)/shard_map/ppermute | solution.py:215
  148.4 2.4 %collective-permute-done.14.across_got = f32[2,32,512]{2,1,0:T(8,128)S(1)} collective-permute-done((f32[2,32,512]{2,1,0:T(8,128)S(1)}, f32[2,32,512]{2,1,0:T(8,128)S(1)}, u32[]{:S(2)}, u32[]{:S(2)}) %collective-permute-start.14) | collective-permute-done | bytes 131104 | tf_op jit(solution)/shard_map/ppermute | solution.py:215
  151.5 3.4 %all-to-all-start.5 = ((f32[4,32,512]{2,1,0:T(8,128)}), f32[4,32,512]{2,1,0:T(8,128)S(1)}, u32[]{:S(2)}, u32[]{:S(2)}) async-start(f32[4,32,512]{2,1,0:T(8,128)} %last.5), calls=%async_computation.5 | async-start | bytes 524288 | tf_op jit(solution)/shard_map/all_to_all | solution.py:228
  155.6 9.2 %all-to-all-done.5.pieces = f32[4,32,512]{2,1,0:T(8,128)S(1)} async-done(((f32[4,32,512]{2,1,0:T(8,128)}), f32[4,32,512]{2,1,0:T(8,128)S(1)}, u32[]{:S(2)}, u32[]{:S(2)}) %all-to-all-start.5) | async-done | bytes 262176 | tf_op jit(solution)/shard_map/all_to_all | solution.py:228
  (37 shorter events, 24.3 us)
Async XLA Ops:
  2.3 21.5 %all-to-all-start = ((f32[8,32,512]{2,1,0:T(8,128)}), f32[8,32,512]{2,1,0:T(8,128)S(1)}, u32[]{:S(2)}, u32[]{:S(2)}) async-start(f32[8,32,512]{2,1,0:T(8,128)} %broadcast_in_dim.10), calls=%async_computation | async-start | bytes 1048576 | tf_op jit(solution)/shard_map/all_to_all | solution.py:244
  23.9 4.0 %copy-start = (bf16[16,8,320,128]{3,2,1,0:T(8,128)(2,1)S(1)}, bf16[16,8,320,128]{3,2,1,0:T(8,128)(2,1)}, u32[]{:S(2)}) copy-start(bf16[16,8,320,128]{3,2,1,0:T(8,128)(2,1)} %prepare.1.mats) | copy-start | bytes 31457284
  23.9 2.0 %collective-permute-start = (f32[8,32,512]{2,1,0:T(8,128)S(1)}, f32[8,32,512]{2,1,0:T(8,128)S(1)}, u32[]{:S(2)}, u32[]{:S(2)}) collective-permute-start(f32[8,32,512]{2,1,0:T(8,128)S(1)} %tie.1.mine), channel_id=1, source_target_pairs={{0,16},{16,0},{1,17},{17,1},{2,18},{18,2},{3,19},{19,3},{4,20},{20... | collective-permute-start | bytes 1572872 | tf_op jit(solution)/shard_map/ppermute | solution.py:215
  29.5 9.1 %collective-permute-start.1 = (f32[4,32,512]{2,1,0:T(8,128)S(1)}, f32[4,32,512]{2,1,0:T(8,128)S(1)}, u32[]{:S(2)}, u32[]{:S(2)}) collective-permute-start(f32[4,32,512]{2,1,0:T(8,128)S(1)} %get-tuple-element.33), channel_id=1, source_target_pairs={{0,8},{8,0},{1,9},{9,1},{2,10},{10,2},{3,11},{11,3},{4,12},{12,4},... | collective-permute-start | bytes 786440 | tf_op jit(solution)/shard_map/ppermute | solution.py:215
  33.9 7.5 %collective-permute-start.2 = (f32[2,2,32,512]{3,2,1,0:T(8,128)S(1)}, f32[2,2,32,512]{3,2,1,0:T(8,128)S(1)}, u32[]{:S(2)}, u32[]{:S(2)}) collective-permute-start(f32[2,2,32,512]{3,2,1,0:T(8,128)S(1)} %second.3), channel_id=1, source_target_pairs={{0,1},{1,0},{2,3},{3,2},{4,5},{5,4},{6,7},{7,6},{8,9},{9,8},{10,11... | collective-permute-start | bytes 786440 | tf_op jit(solution)/shard_map/ppermute | solution.py:215
  37.9 29.5 %copy-start.1 = (f32[32,512]{1,0:T(8,128)S(1)}, f32[32,512]{1,0:T(8,128)}, u32[]{:S(2)}) copy-start(f32[32,512]{1,0:T(8,128)} %before.3) | copy-start | bytes 196612
  37.9 29.5 %copy-start.2 = (f32[512]{0:T(512)S(1)}, f32[512]{0:T(512)}, u32[]{:S(2)}) copy-start(f32[512]{0:T(512)} %param.5) | copy-start | bytes 6148
  42.0 5.1 %collective-permute-start.3 = (f32[2,32,512]{2,1,0:T(8,128)S(1)}, f32[2,32,512]{2,1,0:T(8,128)S(1)}, u32[]{:S(2)}, u32[]{:S(2)}) collective-permute-start(f32[2,32,512]{2,1,0:T(8,128)S(1)} %get-tuple-element.36), channel_id=1, source_target_pairs={{0,1},{1,0},{2,3},{3,2},{4,5},{5,4},{6,7},{7,6},{8,9},{9,8},{10,11... | collective-permute-start | bytes 393224 | tf_op jit(solution)/shard_map/ppermute | solution.py:215
  43.8 6.5 %collective-permute-start.4 = (f32[2,32,512]{2,1,0:T(8,128)S(1)}, f32[2,32,512]{2,1,0:T(8,128)S(1)}, u32[]{:S(2)}, u32[]{:S(2)}) collective-permute-start(f32[2,32,512]{2,1,0:T(8,128)S(1)} %get-tuple-element.38), channel_id=1, source_target_pairs={{0,8},{8,0},{1,9},{9,1},{2,10},{10,2},{3,11},{11,3},{4,12},{12,4},... | collective-permute-start | bytes 393224 | tf_op jit(solution)/shard_map/ppermute | solution.py:215
  79.8 1.9 %collective-permute-start.5 = (f32[8,32,512]{2,1,0:T(8,128)S(1)}, f32[8,32,512]{2,1,0:T(8,128)S(1)}, u32[]{:S(2)}, u32[]{:S(2)}) collective-permute-start(f32[8,32,512]{2,1,0:T(8,128)S(1)} %all_to_all.31.mine), channel_id=1, source_target_pairs={{0,16},{16,0},{1,17},{17,1},{2,18},{18,2},{3,19},{19,3},{4,20},{20... | collective-permute-start | bytes 1572872 | tf_op jit(solution)/shard_map/ppermute | solution.py:215
  83.4 9.9 %collective-permute-start.6 = (f32[4,32,512]{2,1,0:T(8,128)S(1)}, f32[4,32,512]{2,1,0:T(8,128)S(1)}, u32[]{:S(2)}, u32[]{:S(2)}) collective-permute-start(f32[4,32,512]{2,1,0:T(8,128)S(1)} %get-tuple-element.43), channel_id=1, source_target_pairs={{0,8},{8,0},{1,9},{9,1},{2,10},{10,2},{3,11},{11,3},{4,12},{12,4},... | collective-permute-start | bytes 786440 | tf_op jit(solution)/shard_map/ppermute | solution.py:215
  86.7 8.3 %collective-permute-start.7 = (f32[2,2,32,512]{3,2,1,0:T(8,128)S(1)}, f32[2,2,32,512]{3,2,1,0:T(8,128)S(1)}, u32[]{:S(2)}, u32[]{:S(2)}) collective-permute-start(f32[2,2,32,512]{3,2,1,0:T(8,128)S(1)} %second.4), channel_id=1, source_target_pairs={{0,1},{1,0},{2,3},{3,2},{4,5},{5,4},{6,7},{7,6},{8,9},{9,8},{10,11... | collective-permute-start | bytes 786440 | tf_op jit(solution)/shard_map/ppermute | solution.py:215
  95.7 5.1 %collective-permute-start.8 = (f32[2,32,512]{2,1,0:T(8,128)S(1)}, f32[2,32,512]{2,1,0:T(8,128)S(1)}, u32[]{:S(2)}, u32[]{:S(2)}) collective-permute-start(f32[2,32,512]{2,1,0:T(8,128)S(1)} %get-tuple-element.46), channel_id=1, source_target_pairs={{0,1},{1,0},{2,3},{3,2},{4,5},{5,4},{6,7},{7,6},{8,9},{9,8},{10,11... | collective-permute-start | bytes 393224 | tf_op jit(solution)/shard_map/ppermute | solution.py:215
  97.3 6.5 %collective-permute-start.9 = (f32[2,32,512]{2,1,0:T(8,128)S(1)}, f32[2,32,512]{2,1,0:T(8,128)S(1)}, u32[]{:S(2)}, u32[]{:S(2)}) collective-permute-start(f32[2,32,512]{2,1,0:T(8,128)S(1)} %get-tuple-element.48), channel_id=1, source_target_pairs={{0,8},{8,0},{1,9},{9,1},{2,10},{10,2},{3,11},{11,3},{4,12},{12,4},... | collective-permute-start | bytes 393224 | tf_op jit(solution)/shard_map/ppermute | solution.py:215
  127.1 1.9 %collective-permute-start.10 = (f32[8,32,512]{2,1,0:T(8,128)S(1)}, f32[8,32,512]{2,1,0:T(8,128)S(1)}, u32[]{:S(2)}, u32[]{:S(2)}) collective-permute-start(f32[8,32,512]{2,1,0:T(8,128)S(1)} %all_to_all.33.mine), channel_id=1, source_target_pairs={{0,16},{16,0},{1,17},{17,1},{2,18},{18,2},{3,19},{19,3},{4,20},{20... | collective-permute-start | bytes 1572872 | tf_op jit(solution)/shard_map/ppermute | solution.py:215
  130.7 9.9 %collective-permute-start.11 = (f32[4,32,512]{2,1,0:T(8,128)S(1)}, f32[4,32,512]{2,1,0:T(8,128)S(1)}, u32[]{:S(2)}, u32[]{:S(2)}) collective-permute-start(f32[4,32,512]{2,1,0:T(8,128)S(1)} %get-tuple-element.53), channel_id=1, source_target_pairs={{0,8},{8,0},{1,9},{9,1},{2,10},{10,2},{3,11},{11,3},{4,12},{12,4},... | collective-permute-start | bytes 786440 | tf_op jit(solution)/shard_map/ppermute | solution.py:215
  134.6 8.2 %collective-permute-start.12 = (f32[2,2,32,512]{3,2,1,0:T(8,128)S(1)}, f32[2,2,32,512]{3,2,1,0:T(8,128)S(1)}, u32[]{:S(2)}, u32[]{:S(2)}) collective-permute-start(f32[2,2,32,512]{3,2,1,0:T(8,128)S(1)} %second.5), channel_id=1, source_target_pairs={{0,1},{1,0},{2,3},{3,2},{4,5},{5,4},{6,7},{7,6},{8,9},{9,8},{10,11... | collective-permute-start | bytes 786440 | tf_op jit(solution)/shard_map/ppermute | solution.py:215
  143.3 5.1 %collective-permute-start.13 = (f32[2,32,512]{2,1,0:T(8,128)S(1)}, f32[2,32,512]{2,1,0:T(8,128)S(1)}, u32[]{:S(2)}, u32[]{:S(2)}) collective-permute-start(f32[2,32,512]{2,1,0:T(8,128)S(1)} %get-tuple-element.56), channel_id=1, source_target_pairs={{0,1},{1,0},{2,3},{3,2},{4,5},{5,4},{6,7},{7,6},{8,9},{9,8},{10,11... | collective-permute-start | bytes 393224 | tf_op jit(solution)/shard_map/ppermute | solution.py:215
  144.3 6.5 %collective-permute-start.14 = (f32[2,32,512]{2,1,0:T(8,128)S(1)}, f32[2,32,512]{2,1,0:T(8,128)S(1)}, u32[]{:S(2)}, u32[]{:S(2)}) collective-permute-start(f32[2,32,512]{2,1,0:T(8,128)S(1)} %get-tuple-element.58), channel_id=1, source_target_pairs={{0,8},{8,0},{1,9},{9,1},{2,10},{10,2},{3,11},{11,3},{4,12},{12,4},... | collective-permute-start | bytes 393224 | tf_op jit(solution)/shard_map/ppermute | solution.py:215
  151.5 13.3 %all-to-all-start.5 = ((f32[4,32,512]{2,1,0:T(8,128)}), f32[4,32,512]{2,1,0:T(8,128)S(1)}, u32[]{:S(2)}, u32[]{:S(2)}) async-start(f32[4,32,512]{2,1,0:T(8,128)} %last.5), calls=%async_computation.5 | async-start | bytes 524288 | tf_op jit(solution)/shard_map/all_to_all | solution.py:228

commit v3 on v2

v3 whole, which is shorter than its diff:
```python
import functools

import jax
import jax.numpy as jnp
from jax import lax
from jax.experimental import pallas as pl
from jax.experimental.pallas import tpu as pltpu
from jax.sharding import Mesh
from jax.sharding import PartitionSpec as P

BLOCK = 64
DEGREE = 3
LANES = 128
SUB = 8
SLOTS = 5
PAIRS = (SLOTS + 1) // 2
DEPTH = SLOTS * BLOCK
MODES = 32
PER_PIECE = 8
PIECE = BLOCK * PER_PIECE
TILES = PIECE // LANES
ROWS_HERE = 128
HALF_ROW = BLOCK // 2
AT_ONCE = 2

Y_LO, X, CORE, Y_HI, Z_HI, Z_LO = 2, 4, 2, 2, 4, 2
CHIPS = Y_LO * X
Z = Z_HI * Z_LO
CHUNKS = Y_HI * Z
ROW_AXES = ("y_lo", "x", "core")
COL_AXES = ("y_hi", "z_hi", "z_lo")
IN_VMEM = pl.BlockSpec(memory_space=pltpu.VMEM)
IN_SMEM = pl.BlockSpec(memory_space=pltpu.SMEM)


def kept_in_vmem(*shape, dtype=jnp.float32):
    return pltpu.VMEM(shape, dtype)


def call(kernel, name, in_specs, outs, scratch=(), flops=1_000_000, mebibytes=8, **more):
    return pl.pallas_call(
        kernel,
        in_specs=in_specs,
        out_specs=[IN_VMEM] * len(outs),
        out_shape=list(outs),
        scratch_shapes=list(scratch),
        compiler_params=pltpu.CompilerParams(vmem_limit_bytes=mebibytes << 20),
        cost_estimate=pl.CostEstimate(flops=flops, bytes_accessed=100_000, transcendentals=0),
        name=name,
        **more,
    )


def split(value):
    high = value.astype(jnp.bfloat16)
    low = (value - high.astype(jnp.float32)).astype(jnp.bfloat16)
    return high, low


def left_half(shape):
    return lax.broadcasted_iota(jnp.int32, shape, len(shape) - 1) < BLOCK


def prepare_kernel(where, places, *refs):
    *slots, out_ref, rows = refs
    left = left_half((HALF_ROW, LANES))
    down, across = (lax.broadcasted_iota(jnp.int32, (LANES, LANES), dim) for dim in range(2))
    unit = jnp.where(down == across, 1.0, 0.0).astype(jnp.bfloat16)
    for chunk in range(AT_ONCE):
        for row in range(SUB):
            for pair in range(PAIRS):
                first = slots[2 * pair][0, chunk, :, row, :]
                last = 2 * pair + 1 == SLOTS
                second = first if last else slots[2 * pair + 1][0, chunk, :, row, :]
                even = jnp.where(left, first, pltpu.roll(second, BLOCK, 1))
                odd = jnp.where(left, pltpu.roll(first, BLOCK, 1), second)
                slot = (chunk * SUB + row) * PAIRS + pair
                rows[slot, pl.ds(0, HALF_ROW, stride=2), :] = even
                rows[slot, pl.ds(1, HALF_ROW, stride=2), :] = odd
                depth = BLOCK if last else LANES
                turned = lax.dot_general(
                    unit[0:depth],
                    jnp.concatenate(split(rows[slot]), axis=0),
                    (((1,), (1,)), ((), ())),
                    preferred_element_type=jnp.float32,
                )
                out_ref[chunk, row, pl.ds(pair * LANES, depth), :] = turned.astype(jnp.bfloat16)


def slot_spec(slot):
    return pl.BlockSpec((1, AT_ONCE, HALF_ROW, SUB, LANES), lambda g: (slot, g, 0, 0, 0))


def prepare(where, places, coupling):
    raw = coupling.reshape(CHUNKS, SUB, SLOTS, HALF_ROW, LANES).transpose(2, 0, 3, 1, 4)
    raw = pltpu.with_memory_space_constraint(raw, pltpu.HBM)
    return pl.pallas_call(
        prepare_kernel,
        grid=(CHUNKS // AT_ONCE,),
        in_specs=[IN_SMEM, IN_SMEM] + [slot_spec(slot) for slot in range(SLOTS)],
        out_specs=pl.BlockSpec((AT_ONCE, SUB, DEPTH, LANES), lambda g: (g, 0, 0, 0)),
        out_shape=pltpu.HBM((CHUNKS, SUB, DEPTH, LANES), jnp.bfloat16),
        scratch_shapes=[pltpu.VMEM((AT_ONCE * SUB * PAIRS, BLOCK, LANES), jnp.float32)],
        compiler_params=pltpu.CompilerParams(vmem_limit_bytes=16 << 20),
        cost_estimate=pl.CostEstimate(flops=20_000_000_000, bytes_accessed=21 << 20, transcendentals=0),
        name="prepare",
    )(where, places, *[raw] * SLOTS)


def fill_picks(half, ref, picks):
    for chip in range(CHIPS):
        for tile in range(TILES):
            value = ref[chip, :, pl.ds(tile * LANES, LANES)]
            place = (half * CHIPS + chip) * PER_PIECE + 2 * tile
            for turn, turned in enumerate((value, pltpu.roll(value, BLOCK, 1))):
                high, low = split(turned)
                picks[place + turn, 0:MODES, :] = high
                picks[place + turn, MODES : 2 * MODES, :] = low


def fill_kernel(mine, picks):
    fill_picks(0, mine, picks)


def multiply(chunks, stores, places, picks, mats):
    left_picks = left_half((2 * MODES, LANES))
    left_out = left_half((MODES, LANES))
    for chunk, store in zip(chunks, stores):
        previous = None
        for offset in range(SUB):
            row = chunk * SUB + offset
            parts = []
            for pair in range(PAIRS):
                part = picks[places[2 * pair, row]]
                if 2 * pair + 1 < SLOTS:
                    parts.append(jnp.where(left_picks, part, picks[places[2 * pair + 1, row] ^ 1]))
                else:
                    parts.append(part[:, 0:BLOCK])
            product = jnp.dot(jnp.concatenate(parts, axis=1), mats[chunk, offset], preferred_element_type=jnp.float32)
            both = product[0:MODES] + product[MODES : 2 * MODES]
            both = both + pltpu.roll(both, BLOCK, 1)
            if offset % 2 == 1:
                store(pl.ds(offset // 2 * LANES, LANES), jnp.where(left_out, previous, both))
            previous = both


def into(ref, *index):
    def store(lanes, value):
        ref[(*index, slice(None), lanes)] = value

    return store


def multiply_group(where, change, places, picks, mats, out):
    y, low = (where[k] if same == 0 else 1 - where[k] for k, same in enumerate(change))
    chunks = [(y * Z_HI + a) * Z_LO + low for a in range(Z_HI)]
    multiply(chunks, [into(out, a) for a in range(Z_HI)], places, picks, mats)


def first_kernel(change, where, places, half_filled, other, mats, out, picks):
    fill_picks(1, other, picks)
    multiply_group(where, change, places, picks, mats, out)


def next_kernel(change, where, places, picks, mats, out):
    multiply_group(where, change, places, picks, mats, out)


def multiplier(kernel, change, name, inputs, outs, **more):
    return call(
        functools.partial(kernel, change),
        name,
        [IN_SMEM, IN_SMEM] + [IN_VMEM] * (inputs + 1),
        outs,
        flops=100_000,
        **more,
    )


def sum_kernel(where, *refs):
    shares, outs = refs[:-Z_HI], refs[-Z_HI:]
    for ahead, out in enumerate(outs):
        chip = (where[2] + ahead) % Z_HI
        total = shares[0][chip]
        for share in shares[1:]:
            total = total + share[chip]
        out[...] = total


def finish_kernel(scale, energies, vector, before, *refs):
    pieces, (out, *copies) = refs[:Z_HI], refs[Z_HI:]
    total = energies[...] * vector[...]
    for piece in pieces:
        total = total + piece[...]
    if scale != 1.0:
        total = scale * total - before[...]
    out[...] = total
    for ref in copies:
        for chip in range(CHIPS):
            ref[chip] = total


def tie_kernel(mine, mats, out):
    pass


def swap(value, axis):
    return lax.ppermute(value, axis, [(0, 1), (1, 0)])


def shift(value, by):
    return lax.ppermute(value, "z_hi", [(k, (k + by) % Z_HI) for k in range(Z_HI)])


def exchange(value, change):
    pairs = []
    for k in range(Y_HI * Z_LO):
        y, low = k // Z_LO, k % Z_LO
        pairs.append((k, (y ^ change[0]) * Z_LO + (low ^ change[1])))
    return lax.ppermute(value, ("y_hi", "z_lo"), pairs)


def shards(start_modes, energies, coupling, pattern):
    core, y_hi, z_lo = (lax.axis_index(name) for name in ("core", "y_hi", "z_lo"))
    turned = pattern.T
    piece_row = turned // (PER_PIECE * CHUNKS)
    places = (((piece_row % CORE) ^ core) * CHIPS + piece_row // CORE) * PER_PIECE + turned % PER_PIECE
    where = jnp.stack([y_hi, z_lo, lax.axis_index("z_hi")]).astype(jnp.int32)
    mats = prepare(where, places, coupling)
    level = energies[None, :]
    picks_shape = kept_in_vmem(ROWS_HERE, 2 * MODES, LANES, dtype=jnp.bfloat16)
    vector_shape = kept_in_vmem(MODES, PIECE)
    share_shape = kept_in_vmem(Z_HI, MODES, PIECE)

    def operate(copies, tied):
        mine = lax.all_to_all(copies, ("y_lo", "x"), 0, 0, tiled=False)
        if tied:
            [mine] = call(
                tie_kernel, "tie", [IN_VMEM, pl.BlockSpec(memory_space=pl.ANY)], [kept_in_vmem(*mine.shape)], input_output_aliases={0: 0}
            )(mine, pltpu.with_memory_space_constraint(mats, pltpu.HBM))
        other = swap(mine, "core")
        changes = ((1, 1), (1, 0), (0, 1), (0, 0))
        [picks] = call(fill_kernel, "fill", [IN_VMEM], [picks_shape])(mine)
        share, picks = multiplier(
            first_kernel, changes[0], "first", 2, [share_shape, picks_shape], input_output_aliases={2: 1}
        )(where, places, picks, other, mats)
        got = [exchange(share, changes[0])]
        for change in changes[1:]:
            [share] = multiplier(next_kernel, change, "next", 1, [share_shape])(where, places, picks, mats)
            got.append(exchange(share, change) if any(change) else share)
        sums = call(
            sum_kernel,
            "sum",
            [IN_SMEM] + [IN_VMEM] * len(got),
            [vector_shape] * Z_HI,
        )(where, *got)
        return [sums[0]] + [shift(sums[by], by) for by in (2, 1, 3)]

    previous = before = start_modes
    current = start_modes
    copies = jnp.broadcast_to(start_modes[None], (CHIPS, MODES, PIECE))
    for degree in range(DEGREE):
        pieces = operate(copies, degree == 0)
        finish = functools.partial(finish_kernel, 1.0 if degree == 0 else 2.0)
        outs = [vector_shape]
        if degree < DEGREE - 1:
            outs.append(kept_in_vmem(CHIPS, MODES, PIECE))
        upcoming, *rest = call(finish, "finish", [IN_VMEM] * (3 + Z_HI), outs)(level, current, before, *pieces)
        copies = rest[0] if rest else None
        before = current
        current = upcoming
    return (current, before)


def solution(mesh):
    fine = Mesh(mesh.devices.reshape(Y_LO, X, CORE, Y_HI, Z_HI, Z_LO), ROW_AXES + COL_AXES)
    both = ROW_AXES + COL_AXES
    in_specs = (P(None, both), P(both), P(ROW_AXES, COL_AXES, None), P(ROW_AXES, COL_AXES))
    out_specs = (P(None, both), P(None, both))
    return jax.shard_map(shards, mesh=fine, in_specs=in_specs, out_specs=out_specs, check_vma=False)
```

time: 167 us -> 154 us (0.922)
  blocking collectives: 52.8 us -> 26.2 us
  starting transfers between devices: 29.3 us -> 50.2 us
  waiting for transfers between devices: 44.2 us -> 34.2 us
    ppermute x0 -> x18, starting transfers between devices: none -> 44.2 us  [the longest x9 28.3 us: shift(): lax.ppermute(value, 'z_hi', [(k, (k + by) % Z_HI) for k in range(Z_HI)])]
    ppermute x15 -> x3, waiting for transfers between devices: 35 us -> 5.09 us  [swap(): return lax.ppermute(value, axis, [(0, 1), (1, 0)])]
    all_to_all x2 -> x0, blocking collectives: 29.2 us -> none  [reduce(): return lax.all_to_all(sums, 'z_hi', 0, 0, tiled=False)]
    ppermute x0 -> x18, waiting for transfers between devices: none -> 29.1 us  [the longest x9 19.8 us: exchange(): return lax.ppermute(value, ('y_hi', 'z_lo'), pairs)]
    ppermute x15 -> x3, starting transfers between devices: 20.1 us -> 0.1 us  [swap(): return lax.ppermute(value, axis, [(0, 1), (1, 0)])]
    all_to_all x1 -> x0, waiting for transfers between devices: 9.21 us -> none  [reduce(): return lax.all_to_all(sums, 'z_hi', 0, 0, tiled=False)]
    all_to_all x1 -> x0, starting transfers between devices: 3.4 us -> none  [reduce(): return lax.all_to_all(sums, 'z_hi', 0, 0, tiled=False)]
    all_to_all x2, blocking collectives: 23.5 us -> 26.2 us  [operate(): mine = lax.all_to_all(copies, ('y_lo', 'x'), 0, 0, tiled=False)]
  transfers between devices with their start and end apart: 17 -> 22, of which waited for: 16 -> 15; matrix products, arithmetic and copies ran while one was open for 1% -> 1% of each run, Pallas kernels for 15% -> 19%
where the time goes in v3:
time: 154 us; the launch traced here: 152 us
  starting transfers between devices  50.2 us (33%)
  Pallas kernels  35.1 us (23%)
  waiting for transfers between devices  34.2 us (22%)
  blocking collectives  26.2 us (17%)
  local copies, waits for them, and re-layouts  4.94 us (3%)
    ppermute x9, starting transfers between devices, shift(): lax.ppermute(value, 'z_hi', [(k, (k + by) % Z_HI) for k in range(Z_HI)])  28.3 us
    all_to_all x2, blocking collectives, operate(): mine = lax.all_to_all(copies, ('y_lo', 'x'), 0, 0, tiled=False)  26.2 us
    ppermute x9, waiting for transfers between devices, exchange(): return lax.ppermute(value, ('y_hi', 'z_lo'), pairs)  19.8 us
    ppermute x9, starting transfers between devices, exchange(): return lax.ppermute(value, ('y_hi', 'z_lo'), pairs)  15.9 us
    pallas_call x1, Pallas kernels, prepare(): pl.pallas_call(prepare_kernel, grid=(CHUNKS // AT_ONCE,), in_specs=[IN_SM...  14.6 us
    pallas_call x9, Pallas kernels, operate(): multiplier(next_kernel, change, 'next', 1, [share_shape])  13.1 us
    ppermute x9, waiting for transfers between devices, shift(): lax.ppermute(value, 'z_hi', [(k, (k + by) % Z_HI) for k in range(Z_HI)])  9.24 us
    all_to_all x1, starting transfers between devices, operate(): mine = lax.all_to_all(copies, ('y_lo', 'x'), 0, 0, tiled=False)  5.84 us
  transfers between devices with their start and end apart: 22, of which 15 were waited for; matrix products, arithmetic and copies ran while one was open for 1% of the time, Pallas kernels for 19%

profile of v3, /device:TPU:2, one launch (start us, length us, event | category | flops | bytes accessed | tf_op | source)
XLA Modules:
  0.0 152.1 jit_solution(12476481878114493432)
XLA Ops:
  0.6 1.7 %broadcast_in_dim.10 = f32[8,32,512]{2,1,0:T(8,128)} broadcast(f32[32,512]{1,0:T(8,128)} %before.3), dimensions={1,2} | broadcast | bytes 589824 | tf_op jit(solution)/shard_map/broadcast_in_dim | solution.py:261
  2.3 5.8 %all-to-all-start = ((f32[8,32,512]{2,1,0:T(8,128)}), f32[8,32,512]{2,1,0:T(8,128)S(1)}, u32[]{:S(2)}, u32[]{:S(2)}) async-start(f32[8,32,512]{2,1,0:T(8,128)} %broadcast_in_dim.10), calls=%async_computation | async-start | bytes 1048576 | tf_op jit(solution)/shard_map/all_to_all | solution.py:236
  9.0 14.6 %prepare.1.mats = bf16[16,8,320,128]{3,2,1,0:T(8,128)(2,1)} custom-call(s32[3]{0:T(128)S(1)} %pad_add_fusion.where, s32[5,128]{1,0:T(8,128)S(1)} %fusion.5.places, f32[5,16,32,8,128]{4,3,2,1,0:T(8,128)} %bitcast.36, f32[5,16,32,8,128]{4,3,2,1,0:T(8,128)} %bitcast.37, f32[5,16,32,8,128]{4,3,2,1,0:T(8,128)} %bitcast.38, f32[5,16,32,8,128]{4,3,2,1,0:T(8,128)} %bitcast.39, ...), custom_call_target="tpu_custom_call" | custom-call | flops 20000000000 | bytes 22020096 | tf_op jit(solution)/shard_map/prepare/pallas_call | solution.py:97
  23.9 1.7 %collective-permute-done.other = f32[8,32,512]{2,1,0:T(8,128)S(1)} collective-permute-done((f32[8,32,512]{2,1,0:T(8,128)S(1)}, f32[8,32,512]{2,1,0:T(8,128)S(1)}, u32[]{:S(2)}, u32[]{:S(2)}) %collective-permute-start) | collective-permute-done | bytes 524320 | tf_op jit(solution)/shard_map/ppermute | solution.py:208
  25.6 2.0 %copy-done = bf16[16,8,320,128]{3,2,1,0:T(8,128)(2,1)S(1)} copy-done((bf16[16,8,320,128]{3,2,1,0:T(8,128)(2,1)S(1)}, bf16[16,8,320,128]{3,2,1,0:T(8,128)(2,1)}, u32[]{:S(2)}) %copy-start) | copy-done | bytes 10485784
  27.6 1.6 %first.3 = (f32[4,32,512]{2,1,0:T(8,128)S(1)}, bf16[128,64,128]{2,1,0:T(8,128)(2,1)S(1)}) custom-call(s32[3]{0:T(128)S(1)} %pad_add_fusion.where, s32[5,128]{1,0:T(8,128)S(1)} %fusion.5.places, bf16[128,64,128]{2,1,0:T(8,128)(2,1)S(1)} %fill.3.half_filled, f32[8,32,512]{2,1,0:T(8,128)S(1)} %collective-permute-done.other, ...), custom_call_target="tpu_custom_call", output_to_operand_aliasing={{1}: (2, {})} | custom-call | flops 100000 | bytes 100000 | tf_op jit(solution)/shard_map/first/pallas_call | solution.py:244
  29.2 4.3 %collective-permute-start.1 = (f32[4,32,512]{2,1,0:T(8,128)S(1)}, f32[4,32,512]{2,1,0:T(8,128)S(1)}, u32[]{:S(2)}, u32[]{:S(2)}) collective-permute-start(f32[4,32,512]{2,1,0:T(8,128)S(1)} %get-tuple-element.24), channel_id=1, source_target_pairs={{0,9},{1,8},{8,1},{9,0},{2,11},{3,10},{10,3},{11,2},{4,13},{5,12},... | collective-permute-start | bytes 786440 | tf_op jit(solution)/shard_map/ppermute | solution.py:220
  38.8 1.5 %collective-permute-done.1.refs_0_ = f32[4,32,512]{2,1,0:T(8,128)S(1)} collective-permute-done((f32[4,32,512]{2,1,0:T(8,128)S(1)}, f32[4,32,512]{2,1,0:T(8,128)S(1)}, u32[]{:S(2)}, u32[]{:S(2)}) %collective-permute-start.1) | collective-permute-done | bytes 262176 | tf_op jit(solution)/shard_map/ppermute | solution.py:220
  40.3 4.6 %collective-permute-done.2.refs_1_ = f32[4,32,512]{2,1,0:T(8,128)S(1)} collective-permute-done((f32[4,32,512]{2,1,0:T(8,128)S(1)}, f32[4,32,512]{2,1,0:T(8,128)S(1)}, u32[]{:S(2)}, u32[]{:S(2)}) %collective-permute-start.2) | collective-permute-done | bytes 262176 | tf_op jit(solution)/shard_map/ppermute | solution.py:220
  45.5 7.2 %collective-permute-start.4 = (f32[32,512]{1,0:T(8,128)S(1)}, f32[32,512]{1,0:T(8,128)S(1)}, u32[]{:S(2)}, u32[]{:S(2)}) collective-permute-start(f32[32,512]{1,0:T(8,128)S(1)} %get-tuple-element.27), channel_id=1, source_target_pairs={{0,4},{2,6},{4,0},{6,2},{1,5},{3,7},{5,1},{7,3},{8,12},{10,14},{12... | collective-permute-start | bytes 196616 | tf_op jit(solution)/shard_map/ppermute | solution.py:212
  52.7 1.5 collective-permute-start.5
  54.1 2.7 %collective-permute-start.6 = (f32[32,512]{1,0:T(8,128)S(1)}, f32[32,512]{1,0:T(8,128)S(1)}, u32[]{:S(2)}, u32[]{:S(2)}) collective-permute-start(f32[32,512]{1,0:T(8,128)S(1)} %get-tuple-element.29), channel_id=1, source_target_pairs={{0,6},{2,0},{4,2},{6,4},{1,7},{3,1},{5,3},{7,5},{8,14},{10,8},{12,... | collective-permute-start | bytes 196616 | tf_op jit(solution)/shard_map/ppermute | solution.py:212
  56.8 2.4 %collective-permute-done.5.refs_2_ = f32[32,512]{1,0:T(8,128)S(1)} collective-permute-done((f32[32,512]{1,0:T(8,128)S(1)}, f32[32,512]{1,0:T(8,128)S(1)}, u32[]{:S(2)}, u32[]{:S(2)}) %collective-permute-start.5) | collective-permute-done | bytes 65568 | tf_op jit(solution)/shard_map/ppermute | solution.py:212
  59.7 13.6 %all_to_all.15.mine = f32[8,32,512]{2,1,0:T(8,128)S(1)} all-to-all(f32[8,32,512]{2,1,0:T(8,128)S(1)} %get-tuple-element.31), channel_id=1, replica_groups=mesh['y_lo'=2,'x'=4,'core'=2,'y_hi'=2,'z_hi'=4,'z_lo'=2] {'y_lo','x'}, dimensions={0} | all-to-all | bytes 1048576 | tf_op jit(solution)/shard_map/all_to_all | solution.py:236
  73.5 1.7 %collective-permute-done.7.other = f32[8,32,512]{2,1,0:T(8,128)S(1)} collective-permute-done((f32[8,32,512]{2,1,0:T(8,128)S(1)}, f32[8,32,512]{2,1,0:T(8,128)S(1)}, u32[]{:S(2)}, u32[]{:S(2)}) %collective-permute-start.7) | collective-permute-done | bytes 524320 | tf_op jit(solution)/shard_map/ppermute | solution.py:208
  75.2 1.6 %first.4 = (f32[4,32,512]{2,1,0:T(8,128)S(1)}, bf16[128,64,128]{2,1,0:T(8,128)(2,1)S(1)}) custom-call(s32[3]{0:T(128)S(1)} %pad_add_fusion.where, s32[5,128]{1,0:T(8,128)S(1)} %fusion.5.places, bf16[128,64,128]{2,1,0:T(8,128)(2,1)S(1)} %fill.4.half_filled, f32[8,32,512]{2,1,0:T(8,128)S(1)} %collective-permute-done.7.other, ...), custom_call_target="tpu_custom_call", output_to_operand_aliasing={{1}: (2, {})} | custom-call | flops 100000 | bytes 100000 | tf_op jit(solution)/shard_map/first/pallas_call | solution.py:244
  76.8 3.8 %collective-permute-start.8 = (f32[4,32,512]{2,1,0:T(8,128)S(1)}, f32[4,32,512]{2,1,0:T(8,128)S(1)}, u32[]{:S(2)}, u32[]{:S(2)}) collective-permute-start(f32[4,32,512]{2,1,0:T(8,128)S(1)} %get-tuple-element.32), channel_id=1, source_target_pairs={{0,9},{1,8},{8,1},{9,0},{2,11},{3,10},{10,3},{11,2},{4,13},{5,12},... | collective-permute-start | bytes 786440 | tf_op jit(solution)/shard_map/ppermute | solution.py:220
  87.9 5.5 %collective-permute-done.9.refs_1_ = f32[4,32,512]{2,1,0:T(8,128)S(1)} collective-permute-done((f32[4,32,512]{2,1,0:T(8,128)S(1)}, f32[4,32,512]{2,1,0:T(8,128)S(1)}, u32[]{:S(2)}, u32[]{:S(2)}) %collective-permute-start.9) | collective-permute-done | bytes 262176 | tf_op jit(solution)/shard_map/ppermute | solution.py:220
  94.1 5.0 %collective-permute-start.11 = (f32[32,512]{1,0:T(8,128)S(1)}, f32[32,512]{1,0:T(8,128)S(1)}, u32[]{:S(2)}, u32[]{:S(2)}) collective-permute-start(f32[32,512]{1,0:T(8,128)S(1)} %get-tuple-element.35), channel_id=1, source_target_pairs={{0,4},{2,6},{4,0},{6,2},{1,5},{3,7},{5,1},{7,3},{8,12},{10,14},{12... | collective-permute-start | bytes 196616 | tf_op jit(solution)/shard_map/ppermute | solution.py:212
  99.1 1.6 %collective-permute-start.12 = (f32[32,512]{1,0:T(8,128)S(1)}, f32[32,512]{1,0:T(8,128)S(1)}, u32[]{:S(2)}, u32[]{:S(2)}) collective-permute-start(f32[32,512]{1,0:T(8,128)S(1)} %get-tuple-element.36), channel_id=1, source_target_pairs={{0,2},{2,4},{4,6},{6,0},{1,3},{3,5},{5,7},{7,1},{8,10},{10,12},{12... | collective-permute-start | bytes 196616 | tf_op jit(solution)/shard_map/ppermute | solution.py:212
  100.6 2.6 %collective-permute-start.13 = (f32[32,512]{1,0:T(8,128)S(1)}, f32[32,512]{1,0:T(8,128)S(1)}, u32[]{:S(2)}, u32[]{:S(2)}) collective-permute-start(f32[32,512]{1,0:T(8,128)S(1)} %get-tuple-element.37), channel_id=1, source_target_pairs={{0,6},{2,0},{4,2},{6,4},{1,7},{3,1},{5,3},{7,5},{8,14},{10,8},{12,... | collective-permute-start | bytes 196616 | tf_op jit(solution)/shard_map/ppermute | solution.py:212
  103.2 2.3 %collective-permute-done.12.refs_2_ = f32[32,512]{1,0:T(8,128)S(1)} collective-permute-done((f32[32,512]{1,0:T(8,128)S(1)}, f32[32,512]{1,0:T(8,128)S(1)}, u32[]{:S(2)}, u32[]{:S(2)}) %collective-permute-start.12) | collective-permute-done | bytes 65568 | tf_op jit(solution)/shard_map/ppermute | solution.py:212
  106.5 12.6 %all_to_all.16.mine = f32[8,32,512]{2,1,0:T(8,128)S(1)} all-to-all(f32[8,32,512]{2,1,0:T(8,128)S(1)} %get-tuple-element.39), channel_id=1, replica_groups=mesh['y_lo'=2,'x'=4,'core'=2,'y_hi'=2,'z_hi'=4,'z_lo'=2] {'y_lo','x'}, dimensions={0} | all-to-all | bytes 1048576 | tf_op jit(solution)/shard_map/all_to_all | solution.py:236
  119.4 1.7 %collective-permute-done.14.other = f32[8,32,512]{2,1,0:T(8,128)S(1)} collective-permute-done((f32[8,32,512]{2,1,0:T(8,128)S(1)}, f32[8,32,512]{2,1,0:T(8,128)S(1)}, u32[]{:S(2)}, u32[]{:S(2)}) %collective-permute-start.14) | collective-permute-done | bytes 524320 | tf_op jit(solution)/shard_map/ppermute | solution.py:208
  121.1 1.6 %first.5 = (f32[4,32,512]{2,1,0:T(8,128)S(1)}, bf16[128,64,128]{2,1,0:T(8,128)(2,1)S(1)}) custom-call(s32[3]{0:T(128)S(1)} %pad_add_fusion.where, s32[5,128]{1,0:T(8,128)S(1)} %fusion.5.places, bf16[128,64,128]{2,1,0:T(8,128)(2,1)S(1)} %fill.5.half_filled, f32[8,32,512]{2,1,0:T(8,128)S(1)} %collective-permute-done.14.other, ...), custom_call_target="tpu_custom_call", output_to_operand_aliasing={{1}: (2, {})} | custom-call | flops 100000 | bytes 100000 | tf_op jit(solution)/shard_map/first/pallas_call | solution.py:244
  122.7 1.7 %collective-permute-start.15 = (f32[4,32,512]{2,1,0:T(8,128)S(1)}, f32[4,32,512]{2,1,0:T(8,128)S(1)}, u32[]{:S(2)}, u32[]{:S(2)}) collective-permute-start(f32[4,32,512]{2,1,0:T(8,128)S(1)} %get-tuple-element.40), channel_id=1, source_target_pairs={{0,9},{1,8},{8,1},{9,0},{2,11},{3,10},{10,3},{11,2},{4,13},{5,12},... | collective-permute-start | bytes 786440 | tf_op jit(solution)/shard_map/ppermute | solution.py:220
  128.7 2.1 %collective-permute-start.17 = (f32[4,32,512]{2,1,0:T(8,128)S(1)}, f32[4,32,512]{2,1,0:T(8,128)S(1)}, u32[]{:S(2)}, u32[]{:S(2)}) collective-permute-start(f32[4,32,512]{2,1,0:T(8,128)S(1)} %next.16), channel_id=1, source_target_pairs={{0,1},{1,0},{8,9},{9,8},{2,3},{3,2},{10,11},{11,10},{4,5},{5,4},{1... | collective-permute-start | bytes 786440 | tf_op jit(solution)/shard_map/ppermute | solution.py:220
  133.6 5.5 %collective-permute-done.16.refs_1_ = f32[4,32,512]{2,1,0:T(8,128)S(1)} collective-permute-done((f32[4,32,512]{2,1,0:T(8,128)S(1)}, f32[4,32,512]{2,1,0:T(8,128)S(1)}, u32[]{:S(2)}, u32[]{:S(2)}) %collective-permute-start.16) | collective-permute-done | bytes 262176 | tf_op jit(solution)/shard_map/ppermute | solution.py:220
  139.8 3.8 %collective-permute-start.18 = (f32[32,512]{1,0:T(8,128)S(1)}, f32[32,512]{1,0:T(8,128)S(1)}, u32[]{:S(2)}, u32[]{:S(2)}) collective-permute-start(f32[32,512]{1,0:T(8,128)S(1)} %get-tuple-element.43), channel_id=1, source_target_pairs={{0,4},{2,6},{4,0},{6,2},{1,5},{3,7},{5,1},{7,3},{8,12},{10,14},{12... | collective-permute-start | bytes 196616 | tf_op jit(solution)/shard_map/ppermute | solution.py:212
  143.6 1.9 %collective-permute-start.19 = (f32[32,512]{1,0:T(8,128)S(1)}, f32[32,512]{1,0:T(8,128)S(1)}, u32[]{:S(2)}, u32[]{:S(2)}) collective-permute-start(f32[32,512]{1,0:T(8,128)S(1)} %get-tuple-element.44), channel_id=1, source_target_pairs={{0,2},{2,4},{4,6},{6,0},{1,3},{3,5},{5,7},{7,1},{8,10},{10,12},{12... | collective-permute-start | bytes 196616 | tf_op jit(solution)/shard_map/ppermute | solution.py:212
  145.5 2.2 %collective-permute-start.20 = (f32[32,512]{1,0:T(8,128)S(1)}, f32[32,512]{1,0:T(8,128)S(1)}, u32[]{:S(2)}, u32[]{:S(2)}) collective-permute-start(f32[32,512]{1,0:T(8,128)S(1)} %get-tuple-element.45), channel_id=1, source_target_pairs={{0,6},{2,0},{4,2},{6,4},{1,7},{3,1},{5,3},{7,5},{8,14},{10,8},{12,... | collective-permute-start | bytes 196616 | tf_op jit(solution)/shard_map/ppermute | solution.py:212
  148.3 3.1 %collective-permute-done.19.refs_2_ = f32[32,512]{1,0:T(8,128)S(1)} collective-permute-done((f32[32,512]{1,0:T(8,128)S(1)}, f32[32,512]{1,0:T(8,128)S(1)}, u32[]{:S(2)}, u32[]{:S(2)}) %collective-permute-start.19) | collective-permute-done | bytes 65568 | tf_op jit(solution)/shard_map/ppermute | solution.py:212
  (48 shorter events, 25.8 us)
Async XLA Ops:
  2.3 21.3 %all-to-all-start = ((f32[8,32,512]{2,1,0:T(8,128)}), f32[8,32,512]{2,1,0:T(8,128)S(1)}, u32[]{:S(2)}, u32[]{:S(2)}) async-start(f32[8,32,512]{2,1,0:T(8,128)} %broadcast_in_dim.10), calls=%async_computation | async-start | bytes 1048576 | tf_op jit(solution)/shard_map/all_to_all | solution.py:236
  23.6 4.0 %copy-start = (bf16[16,8,320,128]{3,2,1,0:T(8,128)(2,1)S(1)}, bf16[16,8,320,128]{3,2,1,0:T(8,128)(2,1)}, u32[]{:S(2)}) copy-start(bf16[16,8,320,128]{3,2,1,0:T(8,128)(2,1)} %prepare.1.mats) | copy-start | bytes 31457284
  23.6 2.0 %collective-permute-start = (f32[8,32,512]{2,1,0:T(8,128)S(1)}, f32[8,32,512]{2,1,0:T(8,128)S(1)}, u32[]{:S(2)}, u32[]{:S(2)}) collective-permute-start(f32[8,32,512]{2,1,0:T(8,128)S(1)} %tie.1.mine), channel_id=1, source_target_pairs={{0,16},{16,0},{1,17},{17,1},{2,18},{18,2},{3,19},{19,3},{4,20},{20... | collective-permute-start | bytes 1572872 | tf_op jit(solution)/shard_map/ppermute | solution.py:208
  29.2 11.2 %collective-permute-start.1 = (f32[4,32,512]{2,1,0:T(8,128)S(1)}, f32[4,32,512]{2,1,0:T(8,128)S(1)}, u32[]{:S(2)}, u32[]{:S(2)}) collective-permute-start(f32[4,32,512]{2,1,0:T(8,128)S(1)} %get-tuple-element.24), channel_id=1, source_target_pairs={{0,9},{1,8},{8,1},{9,0},{2,11},{3,10},{10,3},{11,2},{4,13},{5,12},... | collective-permute-start | bytes 786440 | tf_op jit(solution)/shard_map/ppermute | solution.py:220
  35.0 9.9 %collective-permute-start.2 = (f32[4,32,512]{2,1,0:T(8,128)S(1)}, f32[4,32,512]{2,1,0:T(8,128)S(1)}, u32[]{:S(2)}, u32[]{:S(2)}) collective-permute-start(f32[4,32,512]{2,1,0:T(8,128)S(1)} %next.9), channel_id=1, source_target_pairs={{0,8},{1,9},{8,0},{9,1},{2,10},{3,11},{10,2},{11,3},{4,12},{5,13},... | collective-permute-start | bytes 786440 | tf_op jit(solution)/shard_map/ppermute | solution.py:220
  37.1 22.5 %copy-start.1 = (f32[32,512]{1,0:T(8,128)S(1)}, f32[32,512]{1,0:T(8,128)}, u32[]{:S(2)}) copy-start(f32[32,512]{1,0:T(8,128)} %before.3) | copy-start | bytes 196612
  37.2 22.5 %copy-start.2 = (f32[512]{0:T(512)S(1)}, f32[512]{0:T(512)}, u32[]{:S(2)}) copy-start(f32[512]{0:T(512)} %param.5) | copy-start | bytes 6148
  37.2 7.7 %collective-permute-start.3 = (f32[4,32,512]{2,1,0:T(8,128)S(1)}, f32[4,32,512]{2,1,0:T(8,128)S(1)}, u32[]{:S(2)}, u32[]{:S(2)}) collective-permute-start(f32[4,32,512]{2,1,0:T(8,128)S(1)} %next.10), channel_id=1, source_target_pairs={{0,1},{1,0},{8,9},{9,8},{2,3},{3,2},{10,11},{11,10},{4,5},{5,4},{1... | collective-permute-start | bytes 786440 | tf_op jit(solution)/shard_map/ppermute | solution.py:220
  45.5 11.3 %collective-permute-start.4 = (f32[32,512]{1,0:T(8,128)S(1)}, f32[32,512]{1,0:T(8,128)S(1)}, u32[]{:S(2)}, u32[]{:S(2)}) collective-permute-start(f32[32,512]{1,0:T(8,128)S(1)} %get-tuple-element.27), channel_id=1, source_target_pairs={{0,4},{2,6},{4,0},{6,2},{1,5},{3,7},{5,1},{7,3},{8,12},{10,14},{12... | collective-permute-start | bytes 196616 | tf_op jit(solution)/shard_map/ppermute | solution.py:212
  52.7 6.6 %collective-permute-start.5 = (f32[32,512]{1,0:T(8,128)S(1)}, f32[32,512]{1,0:T(8,128)S(1)}, u32[]{:S(2)}, u32[]{:S(2)}) collective-permute-start(f32[32,512]{1,0:T(8,128)S(1)} %get-tuple-element.28), channel_id=1, source_target_pairs={{0,2},{2,4},{4,6},{6,0},{1,3},{3,5},{5,7},{7,1},{8,10},{10,12},{12... | collective-permute-start | bytes 196616 | tf_op jit(solution)/shard_map/ppermute | solution.py:212
  54.1 5.5 %collective-permute-start.6 = (f32[32,512]{1,0:T(8,128)S(1)}, f32[32,512]{1,0:T(8,128)S(1)}, u32[]{:S(2)}, u32[]{:S(2)}) collective-permute-start(f32[32,512]{1,0:T(8,128)S(1)} %get-tuple-element.29), channel_id=1, source_target_pairs={{0,6},{2,0},{4,2},{6,4},{1,7},{3,1},{5,3},{7,5},{8,14},{10,8},{12,... | collective-permute-start | bytes 196616 | tf_op jit(solution)/shard_map/ppermute | solution.py:212
  73.3 1.9 %collective-permute-start.7 = (f32[8,32,512]{2,1,0:T(8,128)S(1)}, f32[8,32,512]{2,1,0:T(8,128)S(1)}, u32[]{:S(2)}, u32[]{:S(2)}) collective-permute-start(f32[8,32,512]{2,1,0:T(8,128)S(1)} %all_to_all.15.mine), channel_id=1, source_target_pairs={{0,16},{16,0},{1,17},{17,1},{2,18},{18,2},{3,19},{19,3},{4,20},{20... | collective-permute-start | bytes 1572872 | tf_op jit(solution)/shard_map/ppermute | solution.py:208
  76.8 11.1 %collective-permute-start.8 = (f32[4,32,512]{2,1,0:T(8,128)S(1)}, f32[4,32,512]{2,1,0:T(8,128)S(1)}, u32[]{:S(2)}, u32[]{:S(2)}) collective-permute-start(f32[4,32,512]{2,1,0:T(8,128)S(1)} %get-tuple-element.32), channel_id=1, source_target_pairs={{0,9},{1,8},{8,1},{9,0},{2,11},{3,10},{10,3},{11,2},{4,13},{5,12},... | collective-permute-start | bytes 786440 | tf_op jit(solution)/shard_map/ppermute | solution.py:220
  82.0 11.4 %collective-permute-start.9 = (f32[4,32,512]{2,1,0:T(8,128)S(1)}, f32[4,32,512]{2,1,0:T(8,128)S(1)}, u32[]{:S(2)}, u32[]{:S(2)}) collective-permute-start(f32[4,32,512]{2,1,0:T(8,128)S(1)} %next.12), channel_id=1, source_target_pairs={{0,8},{1,9},{8,0},{9,1},{2,10},{3,11},{10,2},{11,3},{4,12},{5,13},... | collective-permute-start | bytes 786440 | tf_op jit(solution)/shard_map/ppermute | solution.py:220
  84.2 9.4 %collective-permute-start.10 = (f32[4,32,512]{2,1,0:T(8,128)S(1)}, f32[4,32,512]{2,1,0:T(8,128)S(1)}, u32[]{:S(2)}, u32[]{:S(2)}) collective-permute-start(f32[4,32,512]{2,1,0:T(8,128)S(1)} %next.13), channel_id=1, source_target_pairs={{0,1},{1,0},{8,9},{9,8},{2,3},{3,2},{10,11},{11,10},{4,5},{5,4},{1... | collective-permute-start | bytes 786440 | tf_op jit(solution)/shard_map/ppermute | solution.py:220
  94.1 9.1 %collective-permute-start.11 = (f32[32,512]{1,0:T(8,128)S(1)}, f32[32,512]{1,0:T(8,128)S(1)}, u32[]{:S(2)}, u32[]{:S(2)}) collective-permute-start(f32[32,512]{1,0:T(8,128)S(1)} %get-tuple-element.35), channel_id=1, source_target_pairs={{0,4},{2,6},{4,0},{6,2},{1,5},{3,7},{5,1},{7,3},{8,12},{10,14},{12... | collective-permute-start | bytes 196616 | tf_op jit(solution)/shard_map/ppermute | solution.py:212
  99.1 6.5 %collective-permute-start.12 = (f32[32,512]{1,0:T(8,128)S(1)}, f32[32,512]{1,0:T(8,128)S(1)}, u32[]{:S(2)}, u32[]{:S(2)}) collective-permute-start(f32[32,512]{1,0:T(8,128)S(1)} %get-tuple-element.36), channel_id=1, source_target_pairs={{0,2},{2,4},{4,6},{6,0},{1,3},{3,5},{5,7},{7,1},{8,10},{10,12},{12... | collective-permute-start | bytes 196616 | tf_op jit(solution)/shard_map/ppermute | solution.py:212
  100.6 5.9 %collective-permute-start.13 = (f32[32,512]{1,0:T(8,128)S(1)}, f32[32,512]{1,0:T(8,128)S(1)}, u32[]{:S(2)}, u32[]{:S(2)}) collective-permute-start(f32[32,512]{1,0:T(8,128)S(1)} %get-tuple-element.37), channel_id=1, source_target_pairs={{0,6},{2,0},{4,2},{6,4},{1,7},{3,1},{5,3},{7,5},{8,14},{10,8},{12,... | collective-permute-start | bytes 196616 | tf_op jit(solution)/shard_map/ppermute | solution.py:212
  119.2 1.9 %collective-permute-start.14 = (f32[8,32,512]{2,1,0:T(8,128)S(1)}, f32[8,32,512]{2,1,0:T(8,128)S(1)}, u32[]{:S(2)}, u32[]{:S(2)}) collective-permute-start(f32[8,32,512]{2,1,0:T(8,128)S(1)} %all_to_all.16.mine), channel_id=1, source_target_pairs={{0,16},{16,0},{1,17},{17,1},{2,18},{18,2},{3,19},{19,3},{4,20},{20... | collective-permute-start | bytes 1572872 | tf_op jit(solution)/shard_map/ppermute | solution.py:208
  122.7 10.9 %collective-permute-start.15 = (f32[4,32,512]{2,1,0:T(8,128)S(1)}, f32[4,32,512]{2,1,0:T(8,128)S(1)}, u32[]{:S(2)}, u32[]{:S(2)}) collective-permute-start(f32[4,32,512]{2,1,0:T(8,128)S(1)} %get-tuple-element.40), channel_id=1, source_target_pairs={{0,9},{1,8},{8,1},{9,0},{2,11},{3,10},{10,3},{11,2},{4,13},{5,12},... | collective-permute-start | bytes 786440 | tf_op jit(solution)/shard_map/ppermute | solution.py:220
  125.9 13.3 %collective-permute-start.16 = (f32[4,32,512]{2,1,0:T(8,128)S(1)}, f32[4,32,512]{2,1,0:T(8,128)S(1)}, u32[]{:S(2)}, u32[]{:S(2)}) collective-permute-start(f32[4,32,512]{2,1,0:T(8,128)S(1)} %next.15), channel_id=1, source_target_pairs={{0,8},{1,9},{8,0},{9,1},{2,10},{3,11},{10,2},{11,3},{4,12},{5,13},... | collective-permute-start | bytes 786440 | tf_op jit(solution)/shard_map/ppermute | solution.py:220
  128.7 10.4 %collective-permute-start.17 = (f32[4,32,512]{2,1,0:T(8,128)S(1)}, f32[4,32,512]{2,1,0:T(8,128)S(1)}, u32[]{:S(2)}, u32[]{:S(2)}) collective-permute-start(f32[4,32,512]{2,1,0:T(8,128)S(1)} %next.16), channel_id=1, source_target_pairs={{0,1},{1,0},{8,9},{9,8},{2,3},{3,2},{10,11},{11,10},{4,5},{5,4},{1... | collective-permute-start | bytes 786440 | tf_op jit(solution)/shard_map/ppermute | solution.py:220
  139.8 8.6 %collective-permute-start.18 = (f32[32,512]{1,0:T(8,128)S(1)}, f32[32,512]{1,0:T(8,128)S(1)}, u32[]{:S(2)}, u32[]{:S(2)}) collective-permute-start(f32[32,512]{1,0:T(8,128)S(1)} %get-tuple-element.43), channel_id=1, source_target_pairs={{0,4},{2,6},{4,0},{6,2},{1,5},{3,7},{5,1},{7,3},{8,12},{10,14},{12... | collective-permute-start | bytes 196616 | tf_op jit(solution)/shard_map/ppermute | solution.py:212
  143.6 7.9 %collective-permute-start.19 = (f32[32,512]{1,0:T(8,128)S(1)}, f32[32,512]{1,0:T(8,128)S(1)}, u32[]{:S(2)}, u32[]{:S(2)}) collective-permute-start(f32[32,512]{1,0:T(8,128)S(1)} %get-tuple-element.44), channel_id=1, source_target_pairs={{0,2},{2,4},{4,6},{6,0},{1,3},{3,5},{5,7},{7,1},{8,10},{10,12},{12... | collective-permute-start | bytes 196616 | tf_op jit(solution)/shard_map/ppermute | solution.py:212
  145.5 5.9 %collective-permute-start.20 = (f32[32,512]{1,0:T(8,128)S(1)}, f32[32,512]{1,0:T(8,128)S(1)}, u32[]{:S(2)}, u32[]{:S(2)}) collective-permute-start(f32[32,512]{1,0:T(8,128)S(1)} %get-tuple-element.45), channel_id=1, source_target_pairs={{0,6},{2,0},{4,2},{6,4},{1,7},{3,1},{5,3},{7,5},{8,14},{10,8},{12,... | collective-permute-start | bytes 196616 | tf_op jit(solution)/shard_map/ppermute | solution.py:212

commit v4 on v3

--- a/solution.py
+++ b/solution.py
@@ -21,7 +21,7 @@
 TILES = PIECE // LANES
 ROWS_HERE = 128
 HALF_ROW = BLOCK // 2
-AT_ONCE = 2
+AT_ONCE = 4
 
 Y_LO, X, CORE, Y_HI, Z_HI, Z_LO = 2, 4, 2, 2, 4, 2
 CHIPS = Y_LO * X

time: 154 us -> 153 us (level)
  transfers between devices with their start and end apart: 22 -> 22, of which waited for: 15 -> 15; matrix products, arithmetic and copies ran while one was open for 1% -> 1% of each run, Pallas kernels for 19% -> 18%
where the time goes in v4:
time: 153 us; the launch traced here: 151 us
  starting transfers between devices  50.1 us (33%)
  waiting for transfers between devices  34.2 us (22%)
  Pallas kernels  34 us (22%)
  blocking collectives  26.2 us (17%)
  local copies, waits for them, and re-layouts  4.94 us (3%)
    ppermute x9, starting transfers between devices, shift(): lax.ppermute(value, 'z_hi', [(k, (k + by) % Z_HI) for k in range(Z_HI)])  28.3 us
    all_to_all x2, blocking collectives, operate(): mine = lax.all_to_all(copies, ('y_lo', 'x'), 0, 0, tiled=False)  26.2 us
    ppermute x9, waiting for transfers between devices, exchange(): return lax.ppermute(value, ('y_hi', 'z_lo'), pairs)  19.8 us
    ppermute x9, starting transfers between devices, exchange(): return lax.ppermute(value, ('y_hi', 'z_lo'), pairs)  15.9 us
    pallas_call x1, Pallas kernels, prepare(): pl.pallas_call(prepare_kernel, grid=(CHUNKS // AT_ONCE,), in_specs=[IN_SM...  13.5 us
    pallas_call x9, Pallas kernels, operate(): multiplier(next_kernel, change, 'next', 1, [share_shape])  13.1 us
    ppermute x9, waiting for transfers between devices, shift(): lax.ppermute(value, 'z_hi', [(k, (k + by) % Z_HI) for k in range(Z_HI)])  9.33 us
    all_to_all x1, starting transfers between devices, operate(): mine = lax.all_to_all(copies, ('y_lo', 'x'), 0, 0, tiled=False)  5.84 us
  transfers between devices with their start and end apart: 22, of which 15 were waited for; matrix products, arithmetic and copies ran while one was open for 1% of the time, Pallas kernels for 18%

profile of v4, /device:TPU:2, one launch (start us, length us, event | category | flops | bytes accessed | tf_op | source)
XLA Modules:
  0.0 151.1 jit_solution(13425135093972542460)
XLA Ops:
  0.6 1.7 %broadcast_in_dim.10 = f32[8,32,512]{2,1,0:T(8,128)} broadcast(f32[32,512]{1,0:T(8,128)} %before.3), dimensions={1,2} | broadcast | bytes 589824 | tf_op jit(solution)/shard_map/broadcast_in_dim | solution.py:261
  2.3 5.8 %all-to-all-start = ((f32[8,32,512]{2,1,0:T(8,128)}), f32[8,32,512]{2,1,0:T(8,128)S(1)}, u32[]{:S(2)}, u32[]{:S(2)}) async-start(f32[8,32,512]{2,1,0:T(8,128)} %broadcast_in_dim.10), calls=%async_computation | async-start | bytes 1048576 | tf_op jit(solution)/shard_map/all_to_all | solution.py:236
  9.0 13.5 %prepare.1.mats = bf16[16,8,320,128]{3,2,1,0:T(8,128)(2,1)} custom-call(s32[3]{0:T(128)S(1)} %pad_add_fusion.where, s32[5,128]{1,0:T(8,128)S(1)} %fusion.5.places, f32[5,16,32,8,128]{4,3,2,1,0:T(8,128)} %bitcast.36, f32[5,16,32,8,128]{4,3,2,1,0:T(8,128)} %bitcast.37, f32[5,16,32,8,128]{4,3,2,1,0:T(8,128)} %bitcast.38, f32[5,16,32,8,128]{4,3,2,1,0:T(8,128)} %bitcast.39, ...), custom_call_target="tpu_custom_call" | custom-call | flops 20000000000 | bytes 22020096 | tf_op jit(solution)/shard_map/prepare/pallas_call | solution.py:97
  22.8 1.7 %collective-permute-done.other = f32[8,32,512]{2,1,0:T(8,128)S(1)} collective-permute-done((f32[8,32,512]{2,1,0:T(8,128)S(1)}, f32[8,32,512]{2,1,0:T(8,128)S(1)}, u32[]{:S(2)}, u32[]{:S(2)}) %collective-permute-start) | collective-permute-done | bytes 524320 | tf_op jit(solution)/shard_map/ppermute | solution.py:208
  24.5 2.0 %copy-done = bf16[16,8,320,128]{3,2,1,0:T(8,128)(2,1)S(1)} copy-done((bf16[16,8,320,128]{3,2,1,0:T(8,128)(2,1)S(1)}, bf16[16,8,320,128]{3,2,1,0:T(8,128)(2,1)}, u32[]{:S(2)}) %copy-start) | copy-done | bytes 10485784
  26.5 1.6 %first.3 = (f32[4,32,512]{2,1,0:T(8,128)S(1)}, bf16[128,64,128]{2,1,0:T(8,128)(2,1)S(1)}) custom-call(s32[3]{0:T(128)S(1)} %pad_add_fusion.where, s32[5,128]{1,0:T(8,128)S(1)} %fusion.5.places, bf16[128,64,128]{2,1,0:T(8,128)(2,1)S(1)} %fill.3.half_filled, f32[8,32,512]{2,1,0:T(8,128)S(1)} %collective-permute-done.other, ...), custom_call_target="tpu_custom_call", output_to_operand_aliasing={{1}: (2, {})} | custom-call | flops 100000 | bytes 100000 | tf_op jit(solution)/shard_map/first/pallas_call | solution.py:244
  28.1 4.3 %collective-permute-start.1 = (f32[4,32,512]{2,1,0:T(8,128)S(1)}, f32[4,32,512]{2,1,0:T(8,128)S(1)}, u32[]{:S(2)}, u32[]{:S(2)}) collective-permute-start(f32[4,32,512]{2,1,0:T(8,128)S(1)} %get-tuple-element.24), channel_id=1, source_target_pairs={{0,9},{1,8},{8,1},{9,0},{2,11},{3,10},{10,3},{11,2},{4,13},{5,12},... | collective-permute-start | bytes 786440 | tf_op jit(solution)/shard_map/ppermute | solution.py:220
  37.7 1.5 collective-permute-done.1.refs_0_
  39.2 4.6 %collective-permute-done.2.refs_1_ = f32[4,32,512]{2,1,0:T(8,128)S(1)} collective-permute-done((f32[4,32,512]{2,1,0:T(8,128)S(1)}, f32[4,32,512]{2,1,0:T(8,128)S(1)}, u32[]{:S(2)}, u32[]{:S(2)}) %collective-permute-start.2) | collective-permute-done | bytes 262176 | tf_op jit(solution)/shard_map/ppermute | solution.py:220
  44.4 7.2 %collective-permute-start.4 = (f32[32,512]{1,0:T(8,128)S(1)}, f32[32,512]{1,0:T(8,128)S(1)}, u32[]{:S(2)}, u32[]{:S(2)}) collective-permute-start(f32[32,512]{1,0:T(8,128)S(1)} %get-tuple-element.27), channel_id=1, source_target_pairs={{0,4},{2,6},{4,0},{6,2},{1,5},{3,7},{5,1},{7,3},{8,12},{10,14},{12... | collective-permute-start | bytes 196616 | tf_op jit(solution)/shard_map/ppermute | solution.py:212
  51.6 1.5 collective-permute-start.5
  53.0 2.7 %collective-permute-start.6 = (f32[32,512]{1,0:T(8,128)S(1)}, f32[32,512]{1,0:T(8,128)S(1)}, u32[]{:S(2)}, u32[]{:S(2)}) collective-permute-start(f32[32,512]{1,0:T(8,128)S(1)} %get-tuple-element.29), channel_id=1, source_target_pairs={{0,6},{2,0},{4,2},{6,4},{1,7},{3,1},{5,3},{7,5},{8,14},{10,8},{12,... | collective-permute-start | bytes 196616 | tf_op jit(solution)/shard_map/ppermute | solution.py:212
  55.7 2.4 %collective-permute-done.5.refs_2_ = f32[32,512]{1,0:T(8,128)S(1)} collective-permute-done((f32[32,512]{1,0:T(8,128)S(1)}, f32[32,512]{1,0:T(8,128)S(1)}, u32[]{:S(2)}, u32[]{:S(2)}) %collective-permute-start.5) | collective-permute-done | bytes 65568 | tf_op jit(solution)/shard_map/ppermute | solution.py:212
  58.6 13.6 %all_to_all.15.mine = f32[8,32,512]{2,1,0:T(8,128)S(1)} all-to-all(f32[8,32,512]{2,1,0:T(8,128)S(1)} %get-tuple-element.31), channel_id=1, replica_groups=mesh['y_lo'=2,'x'=4,'core'=2,'y_hi'=2,'z_hi'=4,'z_lo'=2] {'y_lo','x'}, dimensions={0} | all-to-all | bytes 1048576 | tf_op jit(solution)/shard_map/all_to_all | solution.py:236
  72.4 1.7 %collective-permute-done.7.other = f32[8,32,512]{2,1,0:T(8,128)S(1)} collective-permute-done((f32[8,32,512]{2,1,0:T(8,128)S(1)}, f32[8,32,512]{2,1,0:T(8,128)S(1)}, u32[]{:S(2)}, u32[]{:S(2)}) %collective-permute-start.7) | collective-permute-done | bytes 524320 | tf_op jit(solution)/shard_map/ppermute | solution.py:208
  74.1 1.6 %first.4 = (f32[4,32,512]{2,1,0:T(8,128)S(1)}, bf16[128,64,128]{2,1,0:T(8,128)(2,1)S(1)}) custom-call(s32[3]{0:T(128)S(1)} %pad_add_fusion.where, s32[5,128]{1,0:T(8,128)S(1)} %fusion.5.places, bf16[128,64,128]{2,1,0:T(8,128)(2,1)S(1)} %fill.4.half_filled, f32[8,32,512]{2,1,0:T(8,128)S(1)} %collective-permute-done.7.other, ...), custom_call_target="tpu_custom_call", output_to_operand_aliasing={{1}: (2, {})} | custom-call | flops 100000 | bytes 100000 | tf_op jit(solution)/shard_map/first/pallas_call | solution.py:244
  75.7 3.8 %collective-permute-start.8 = (f32[4,32,512]{2,1,0:T(8,128)S(1)}, f32[4,32,512]{2,1,0:T(8,128)S(1)}, u32[]{:S(2)}, u32[]{:S(2)}) collective-permute-start(f32[4,32,512]{2,1,0:T(8,128)S(1)} %get-tuple-element.32), channel_id=1, source_target_pairs={{0,9},{1,8},{8,1},{9,0},{2,11},{3,10},{10,3},{11,2},{4,13},{5,12},... | collective-permute-start | bytes 786440 | tf_op jit(solution)/shard_map/ppermute | solution.py:220
  86.8 5.5 %collective-permute-done.9.refs_1_ = f32[4,32,512]{2,1,0:T(8,128)S(1)} collective-permute-done((f32[4,32,512]{2,1,0:T(8,128)S(1)}, f32[4,32,512]{2,1,0:T(8,128)S(1)}, u32[]{:S(2)}, u32[]{:S(2)}) %collective-permute-start.9) | collective-permute-done | bytes 262176 | tf_op jit(solution)/shard_map/ppermute | solution.py:220
  93.0 4.9 %collective-permute-start.11 = (f32[32,512]{1,0:T(8,128)S(1)}, f32[32,512]{1,0:T(8,128)S(1)}, u32[]{:S(2)}, u32[]{:S(2)}) collective-permute-start(f32[32,512]{1,0:T(8,128)S(1)} %get-tuple-element.35), channel_id=1, source_target_pairs={{0,4},{2,6},{4,0},{6,2},{1,5},{3,7},{5,1},{7,3},{8,12},{10,14},{12... | collective-permute-start | bytes 196616 | tf_op jit(solution)/shard_map/ppermute | solution.py:212
  98.0 1.6 %collective-permute-start.12 = (f32[32,512]{1,0:T(8,128)S(1)}, f32[32,512]{1,0:T(8,128)S(1)}, u32[]{:S(2)}, u32[]{:S(2)}) collective-permute-start(f32[32,512]{1,0:T(8,128)S(1)} %get-tuple-element.36), channel_id=1, source_target_pairs={{0,2},{2,4},{4,6},{6,0},{1,3},{3,5},{5,7},{7,1},{8,10},{10,12},{12... | collective-permute-start | bytes 196616 | tf_op jit(solution)/shard_map/ppermute | solution.py:212
  99.5 2.6 %collective-permute-start.13 = (f32[32,512]{1,0:T(8,128)S(1)}, f32[32,512]{1,0:T(8,128)S(1)}, u32[]{:S(2)}, u32[]{:S(2)}) collective-permute-start(f32[32,512]{1,0:T(8,128)S(1)} %get-tuple-element.37), channel_id=1, source_target_pairs={{0,6},{2,0},{4,2},{6,4},{1,7},{3,1},{5,3},{7,5},{8,14},{10,8},{12,... | collective-permute-start | bytes 196616 | tf_op jit(solution)/shard_map/ppermute | solution.py:212
  102.1 2.3 %collective-permute-done.12.refs_2_ = f32[32,512]{1,0:T(8,128)S(1)} collective-permute-done((f32[32,512]{1,0:T(8,128)S(1)}, f32[32,512]{1,0:T(8,128)S(1)}, u32[]{:S(2)}, u32[]{:S(2)}) %collective-permute-start.12) | collective-permute-done | bytes 65568 | tf_op jit(solution)/shard_map/ppermute | solution.py:212
  105.5 12.6 %all_to_all.16.mine = f32[8,32,512]{2,1,0:T(8,128)S(1)} all-to-all(f32[8,32,512]{2,1,0:T(8,128)S(1)} %get-tuple-element.39), channel_id=1, replica_groups=mesh['y_lo'=2,'x'=4,'core'=2,'y_hi'=2,'z_hi'=4,'z_lo'=2] {'y_lo','x'}, dimensions={0} | all-to-all | bytes 1048576 | tf_op jit(solution)/shard_map/all_to_all | solution.py:236
  118.3 1.7 %collective-permute-done.14.other = f32[8,32,512]{2,1,0:T(8,128)S(1)} collective-permute-done((f32[8,32,512]{2,1,0:T(8,128)S(1)}, f32[8,32,512]{2,1,0:T(8,128)S(1)}, u32[]{:S(2)}, u32[]{:S(2)}) %collective-permute-start.14) | collective-permute-done | bytes 524320 | tf_op jit(solution)/shard_map/ppermute | solution.py:208
  120.0 1.6 %first.5 = (f32[4,32,512]{2,1,0:T(8,128)S(1)}, bf16[128,64,128]{2,1,0:T(8,128)(2,1)S(1)}) custom-call(s32[3]{0:T(128)S(1)} %pad_add_fusion.where, s32[5,128]{1,0:T(8,128)S(1)} %fusion.5.places, bf16[128,64,128]{2,1,0:T(8,128)(2,1)S(1)} %fill.5.half_filled, f32[8,32,512]{2,1,0:T(8,128)S(1)} %collective-permute-done.14.other, ...), custom_call_target="tpu_custom_call", output_to_operand_aliasing={{1}: (2, {})} | custom-call | flops 100000 | bytes 100000 | tf_op jit(solution)/shard_map/first/pallas_call | solution.py:244
  121.6 1.7 %collective-permute-start.15 = (f32[4,32,512]{2,1,0:T(8,128)S(1)}, f32[4,32,512]{2,1,0:T(8,128)S(1)}, u32[]{:S(2)}, u32[]{:S(2)}) collective-permute-start(f32[4,32,512]{2,1,0:T(8,128)S(1)} %get-tuple-element.40), channel_id=1, source_target_pairs={{0,9},{1,8},{8,1},{9,0},{2,11},{3,10},{10,3},{11,2},{4,13},{5,12},... | collective-permute-start | bytes 786440 | tf_op jit(solution)/shard_map/ppermute | solution.py:220
  127.6 2.2 %collective-permute-start.17 = (f32[4,32,512]{2,1,0:T(8,128)S(1)}, f32[4,32,512]{2,1,0:T(8,128)S(1)}, u32[]{:S(2)}, u32[]{:S(2)}) collective-permute-start(f32[4,32,512]{2,1,0:T(8,128)S(1)} %next.16), channel_id=1, source_target_pairs={{0,1},{1,0},{8,9},{9,8},{2,3},{3,2},{10,11},{11,10},{4,5},{5,4},{1... | collective-permute-start | bytes 786440 | tf_op jit(solution)/shard_map/ppermute | solution.py:220
  132.6 5.5 %collective-permute-done.16.refs_1_ = f32[4,32,512]{2,1,0:T(8,128)S(1)} collective-permute-done((f32[4,32,512]{2,1,0:T(8,128)S(1)}, f32[4,32,512]{2,1,0:T(8,128)S(1)}, u32[]{:S(2)}, u32[]{:S(2)}) %collective-permute-start.16) | collective-permute-done | bytes 262176 | tf_op jit(solution)/shard_map/ppermute | solution.py:220
  138.7 3.8 %collective-permute-start.18 = (f32[32,512]{1,0:T(8,128)S(1)}, f32[32,512]{1,0:T(8,128)S(1)}, u32[]{:S(2)}, u32[]{:S(2)}) collective-permute-start(f32[32,512]{1,0:T(8,128)S(1)} %get-tuple-element.43), channel_id=1, source_target_pairs={{0,4},{2,6},{4,0},{6,2},{1,5},{3,7},{5,1},{7,3},{8,12},{10,14},{12... | collective-permute-start | bytes 196616 | tf_op jit(solution)/shard_map/ppermute | solution.py:212
  142.5 2.0 %collective-permute-start.19 = (f32[32,512]{1,0:T(8,128)S(1)}, f32[32,512]{1,0:T(8,128)S(1)}, u32[]{:S(2)}, u32[]{:S(2)}) collective-permute-start(f32[32,512]{1,0:T(8,128)S(1)} %get-tuple-element.44), channel_id=1, source_target_pairs={{0,2},{2,4},{4,6},{6,0},{1,3},{3,5},{5,7},{7,1},{8,10},{10,12},{12... | collective-permute-start | bytes 196616 | tf_op jit(solution)/shard_map/ppermute | solution.py:212
  144.4 2.2 %collective-permute-start.20 = (f32[32,512]{1,0:T(8,128)S(1)}, f32[32,512]{1,0:T(8,128)S(1)}, u32[]{:S(2)}, u32[]{:S(2)}) collective-permute-start(f32[32,512]{1,0:T(8,128)S(1)} %get-tuple-element.45), channel_id=1, source_target_pairs={{0,6},{2,0},{4,2},{6,4},{1,7},{3,1},{5,3},{7,5},{8,14},{10,8},{12,... | collective-permute-start | bytes 196616 | tf_op jit(solution)/shard_map/ppermute | solution.py:212
  147.2 3.2 %collective-permute-done.19.refs_2_ = f32[32,512]{1,0:T(8,128)S(1)} collective-permute-done((f32[32,512]{1,0:T(8,128)S(1)}, f32[32,512]{1,0:T(8,128)S(1)}, u32[]{:S(2)}, u32[]{:S(2)}) %collective-permute-start.19) | collective-permute-done | bytes 65568 | tf_op jit(solution)/shard_map/ppermute | solution.py:212
  (48 shorter events, 25.9 us)
Async XLA Ops:
  2.3 20.2 %all-to-all-start = ((f32[8,32,512]{2,1,0:T(8,128)}), f32[8,32,512]{2,1,0:T(8,128)S(1)}, u32[]{:S(2)}, u32[]{:S(2)}) async-start(f32[8,32,512]{2,1,0:T(8,128)} %broadcast_in_dim.10), calls=%async_computation | async-start | bytes 1048576 | tf_op jit(solution)/shard_map/all_to_all | solution.py:236
  22.5 4.0 %copy-start = (bf16[16,8,320,128]{3,2,1,0:T(8,128)(2,1)S(1)}, bf16[16,8,320,128]{3,2,1,0:T(8,128)(2,1)}, u32[]{:S(2)}) copy-start(bf16[16,8,320,128]{3,2,1,0:T(8,128)(2,1)} %prepare.1.mats) | copy-start | bytes 31457284
  22.5 2.0 %collective-permute-start = (f32[8,32,512]{2,1,0:T(8,128)S(1)}, f32[8,32,512]{2,1,0:T(8,128)S(1)}, u32[]{:S(2)}, u32[]{:S(2)}) collective-permute-start(f32[8,32,512]{2,1,0:T(8,128)S(1)} %tie.1.mine), channel_id=1, source_target_pairs={{0,16},{16,0},{1,17},{17,1},{2,18},{18,2},{3,19},{19,3},{4,20},{20... | collective-permute-start | bytes 1572872 | tf_op jit(solution)/shard_map/ppermute | solution.py:208
  28.1 11.1 %collective-permute-start.1 = (f32[4,32,512]{2,1,0:T(8,128)S(1)}, f32[4,32,512]{2,1,0:T(8,128)S(1)}, u32[]{:S(2)}, u32[]{:S(2)}) collective-permute-start(f32[4,32,512]{2,1,0:T(8,128)S(1)} %get-tuple-element.24), channel_id=1, source_target_pairs={{0,9},{1,8},{8,1},{9,0},{2,11},{3,10},{10,3},{11,2},{4,13},{5,12},... | collective-permute-start | bytes 786440 | tf_op jit(solution)/shard_map/ppermute | solution.py:220
  33.9 9.9 %collective-permute-start.2 = (f32[4,32,512]{2,1,0:T(8,128)S(1)}, f32[4,32,512]{2,1,0:T(8,128)S(1)}, u32[]{:S(2)}, u32[]{:S(2)}) collective-permute-start(f32[4,32,512]{2,1,0:T(8,128)S(1)} %next.9), channel_id=1, source_target_pairs={{0,8},{1,9},{8,0},{9,1},{2,10},{3,11},{10,2},{11,3},{4,12},{5,13},... | collective-permute-start | bytes 786440 | tf_op jit(solution)/shard_map/ppermute | solution.py:220
  36.0 22.5 %copy-start.1 = (f32[32,512]{1,0:T(8,128)S(1)}, f32[32,512]{1,0:T(8,128)}, u32[]{:S(2)}) copy-start(f32[32,512]{1,0:T(8,128)} %before.3) | copy-start | bytes 196612
  36.1 22.5 %copy-start.2 = (f32[512]{0:T(512)S(1)}, f32[512]{0:T(512)}, u32[]{:S(2)}) copy-start(f32[512]{0:T(512)} %param.5) | copy-start | bytes 6148
  36.1 7.7 %collective-permute-start.3 = (f32[4,32,512]{2,1,0:T(8,128)S(1)}, f32[4,32,512]{2,1,0:T(8,128)S(1)}, u32[]{:S(2)}, u32[]{:S(2)}) collective-permute-start(f32[4,32,512]{2,1,0:T(8,128)S(1)} %next.10), channel_id=1, source_target_pairs={{0,1},{1,0},{8,9},{9,8},{2,3},{3,2},{10,11},{11,10},{4,5},{5,4},{1... | collective-permute-start | bytes 786440 | tf_op jit(solution)/shard_map/ppermute | solution.py:220
  44.4 11.3 %collective-permute-start.4 = (f32[32,512]{1,0:T(8,128)S(1)}, f32[32,512]{1,0:T(8,128)S(1)}, u32[]{:S(2)}, u32[]{:S(2)}) collective-permute-start(f32[32,512]{1,0:T(8,128)S(1)} %get-tuple-element.27), channel_id=1, source_target_pairs={{0,4},{2,6},{4,0},{6,2},{1,5},{3,7},{5,1},{7,3},{8,12},{10,14},{12... | collective-permute-start | bytes 196616 | tf_op jit(solution)/shard_map/ppermute | solution.py:212
  51.6 6.6 %collective-permute-start.5 = (f32[32,512]{1,0:T(8,128)S(1)}, f32[32,512]{1,0:T(8,128)S(1)}, u32[]{:S(2)}, u32[]{:S(2)}) collective-permute-start(f32[32,512]{1,0:T(8,128)S(1)} %get-tuple-element.28), channel_id=1, source_target_pairs={{0,2},{2,4},{4,6},{6,0},{1,3},{3,5},{5,7},{7,1},{8,10},{10,12},{12... | collective-permute-start | bytes 196616 | tf_op jit(solution)/shard_map/ppermute | solution.py:212
  53.0 5.5 %collective-permute-start.6 = (f32[32,512]{1,0:T(8,128)S(1)}, f32[32,512]{1,0:T(8,128)S(1)}, u32[]{:S(2)}, u32[]{:S(2)}) collective-permute-start(f32[32,512]{1,0:T(8,128)S(1)} %get-tuple-element.29), channel_id=1, source_target_pairs={{0,6},{2,0},{4,2},{6,4},{1,7},{3,1},{5,3},{7,5},{8,14},{10,8},{12,... | collective-permute-start | bytes 196616 | tf_op jit(solution)/shard_map/ppermute | solution.py:212
  72.2 1.9 %collective-permute-start.7 = (f32[8,32,512]{2,1,0:T(8,128)S(1)}, f32[8,32,512]{2,1,0:T(8,128)S(1)}, u32[]{:S(2)}, u32[]{:S(2)}) collective-permute-start(f32[8,32,512]{2,1,0:T(8,128)S(1)} %all_to_all.15.mine), channel_id=1, source_target_pairs={{0,16},{16,0},{1,17},{17,1},{2,18},{18,2},{3,19},{19,3},{4,20},{20... | collective-permute-start | bytes 1572872 | tf_op jit(solution)/shard_map/ppermute | solution.py:208
  75.7 11.1 %collective-permute-start.8 = (f32[4,32,512]{2,1,0:T(8,128)S(1)}, f32[4,32,512]{2,1,0:T(8,128)S(1)}, u32[]{:S(2)}, u32[]{:S(2)}) collective-permute-start(f32[4,32,512]{2,1,0:T(8,128)S(1)} %get-tuple-element.32), channel_id=1, source_target_pairs={{0,9},{1,8},{8,1},{9,0},{2,11},{3,10},{10,3},{11,2},{4,13},{5,12},... | collective-permute-start | bytes 786440 | tf_op jit(solution)/shard_map/ppermute | solution.py:220
  80.9 11.4 %collective-permute-start.9 = (f32[4,32,512]{2,1,0:T(8,128)S(1)}, f32[4,32,512]{2,1,0:T(8,128)S(1)}, u32[]{:S(2)}, u32[]{:S(2)}) collective-permute-start(f32[4,32,512]{2,1,0:T(8,128)S(1)} %next.12), channel_id=1, source_target_pairs={{0,8},{1,9},{8,0},{9,1},{2,10},{3,11},{10,2},{11,3},{4,12},{5,13},... | collective-permute-start | bytes 786440 | tf_op jit(solution)/shard_map/ppermute | solution.py:220
  83.1 9.4 %collective-permute-start.10 = (f32[4,32,512]{2,1,0:T(8,128)S(1)}, f32[4,32,512]{2,1,0:T(8,128)S(1)}, u32[]{:S(2)}, u32[]{:S(2)}) collective-permute-start(f32[4,32,512]{2,1,0:T(8,128)S(1)} %next.13), channel_id=1, source_target_pairs={{0,1},{1,0},{8,9},{9,8},{2,3},{3,2},{10,11},{11,10},{4,5},{5,4},{1... | collective-permute-start | bytes 786440 | tf_op jit(solution)/shard_map/ppermute | solution.py:220
  93.0 9.1 %collective-permute-start.11 = (f32[32,512]{1,0:T(8,128)S(1)}, f32[32,512]{1,0:T(8,128)S(1)}, u32[]{:S(2)}, u32[]{:S(2)}) collective-permute-start(f32[32,512]{1,0:T(8,128)S(1)} %get-tuple-element.35), channel_id=1, source_target_pairs={{0,4},{2,6},{4,0},{6,2},{1,5},{3,7},{5,1},{7,3},{8,12},{10,14},{12... | collective-permute-start | bytes 196616 | tf_op jit(solution)/shard_map/ppermute | solution.py:212
  98.0 6.5 %collective-permute-start.12 = (f32[32,512]{1,0:T(8,128)S(1)}, f32[32,512]{1,0:T(8,128)S(1)}, u32[]{:S(2)}, u32[]{:S(2)}) collective-permute-start(f32[32,512]{1,0:T(8,128)S(1)} %get-tuple-element.36), channel_id=1, source_target_pairs={{0,2},{2,4},{4,6},{6,0},{1,3},{3,5},{5,7},{7,1},{8,10},{10,12},{12... | collective-permute-start | bytes 196616 | tf_op jit(solution)/shard_map/ppermute | solution.py:212
  99.5 5.9 %collective-permute-start.13 = (f32[32,512]{1,0:T(8,128)S(1)}, f32[32,512]{1,0:T(8,128)S(1)}, u32[]{:S(2)}, u32[]{:S(2)}) collective-permute-start(f32[32,512]{1,0:T(8,128)S(1)} %get-tuple-element.37), channel_id=1, source_target_pairs={{0,6},{2,0},{4,2},{6,4},{1,7},{3,1},{5,3},{7,5},{8,14},{10,8},{12,... | collective-permute-start | bytes 196616 | tf_op jit(solution)/shard_map/ppermute | solution.py:212
  118.1 1.9 %collective-permute-start.14 = (f32[8,32,512]{2,1,0:T(8,128)S(1)}, f32[8,32,512]{2,1,0:T(8,128)S(1)}, u32[]{:S(2)}, u32[]{:S(2)}) collective-permute-start(f32[8,32,512]{2,1,0:T(8,128)S(1)} %all_to_all.16.mine), channel_id=1, source_target_pairs={{0,16},{16,0},{1,17},{17,1},{2,18},{18,2},{3,19},{19,3},{4,20},{20... | collective-permute-start | bytes 1572872 | tf_op jit(solution)/shard_map/ppermute | solution.py:208
  121.6 10.9 %collective-permute-start.15 = (f32[4,32,512]{2,1,0:T(8,128)S(1)}, f32[4,32,512]{2,1,0:T(8,128)S(1)}, u32[]{:S(2)}, u32[]{:S(2)}) collective-permute-start(f32[4,32,512]{2,1,0:T(8,128)S(1)} %get-tuple-element.40), channel_id=1, source_target_pairs={{0,9},{1,8},{8,1},{9,0},{2,11},{3,10},{10,3},{11,2},{4,13},{5,12},... | collective-permute-start | bytes 786440 | tf_op jit(solution)/shard_map/ppermute | solution.py:220
  124.8 13.3 %collective-permute-start.16 = (f32[4,32,512]{2,1,0:T(8,128)S(1)}, f32[4,32,512]{2,1,0:T(8,128)S(1)}, u32[]{:S(2)}, u32[]{:S(2)}) collective-permute-start(f32[4,32,512]{2,1,0:T(8,128)S(1)} %next.15), channel_id=1, source_target_pairs={{0,8},{1,9},{8,0},{9,1},{2,10},{3,11},{10,2},{11,3},{4,12},{5,13},... | collective-permute-start | bytes 786440 | tf_op jit(solution)/shard_map/ppermute | solution.py:220
  127.6 10.5 %collective-permute-start.17 = (f32[4,32,512]{2,1,0:T(8,128)S(1)}, f32[4,32,512]{2,1,0:T(8,128)S(1)}, u32[]{:S(2)}, u32[]{:S(2)}) collective-permute-start(f32[4,32,512]{2,1,0:T(8,128)S(1)} %next.16), channel_id=1, source_target_pairs={{0,1},{1,0},{8,9},{9,8},{2,3},{3,2},{10,11},{11,10},{4,5},{5,4},{1... | collective-permute-start | bytes 786440 | tf_op jit(solution)/shard_map/ppermute | solution.py:220
  138.7 8.5 %collective-permute-start.18 = (f32[32,512]{1,0:T(8,128)S(1)}, f32[32,512]{1,0:T(8,128)S(1)}, u32[]{:S(2)}, u32[]{:S(2)}) collective-permute-start(f32[32,512]{1,0:T(8,128)S(1)} %get-tuple-element.43), channel_id=1, source_target_pairs={{0,4},{2,6},{4,0},{6,2},{1,5},{3,7},{5,1},{7,3},{8,12},{10,14},{12... | collective-permute-start | bytes 196616 | tf_op jit(solution)/shard_map/ppermute | solution.py:212
  142.5 7.9 %collective-permute-start.19 = (f32[32,512]{1,0:T(8,128)S(1)}, f32[32,512]{1,0:T(8,128)S(1)}, u32[]{:S(2)}, u32[]{:S(2)}) collective-permute-start(f32[32,512]{1,0:T(8,128)S(1)} %get-tuple-element.44), channel_id=1, source_target_pairs={{0,2},{2,4},{4,6},{6,0},{1,3},{3,5},{5,7},{7,1},{8,10},{10,12},{12... | collective-permute-start | bytes 196616 | tf_op jit(solution)/shard_map/ppermute | solution.py:212
  144.4 6.0 %collective-permute-start.20 = (f32[32,512]{1,0:T(8,128)S(1)}, f32[32,512]{1,0:T(8,128)S(1)}, u32[]{:S(2)}, u32[]{:S(2)}) collective-permute-start(f32[32,512]{1,0:T(8,128)S(1)} %get-tuple-element.45), channel_id=1, source_target_pairs={{0,6},{2,0},{4,2},{6,4},{1,7},{3,1},{5,3},{7,5},{8,14},{10,8},{12,... | collective-permute-start | bytes 196616 | tf_op jit(solution)/shard_map/ppermute | solution.py:212
